TPU v7x, 32 devices: a whole 2x2x4 slice. The times are simulated.
32 devices in a mesh: tm: 2 (over x), space: 16 (over z, y, core).
Axes of the slice: x: 2, y: 2, z: 4, core: 2. Of those that a mesh axis runs over, the one named last changes fastest.
Arguments:
- states: float32 [4, 128, 64, 128], P('tm', 'space'), may hold values from -1.2 to 1.2
- kappa: float32 [128, 64, 128], P('space'), may hold values from 0.02 to 0.15
- rate: float32 [128, 64, 128], P('space'), may hold values from 0.02 to 0.2
Outputs:
- ends: float32 [4, 128, 64, 128], P('tm', 'space')
All inputs are finite; a program needn't handle non-finite values.
Results may differ from a plain program's by a relative error of at most 0.00013.
Values sent between devices are 32-bit elements; how exact they have to be, the bound alone decides.
A program may use at most 64 MiB of HBM per device.

v0:
```python
import jax
import jax.numpy as jnp
from jax import lax
from jax.sharding import PartitionSpec as P

STEPS = 12


def extended_2(cells, sides, width):
    for axis, dim in sides:
        count = lax.axis_size(axis)
        ends = count - 1
        head = lax.slice_in_dim(cells, 0, width, axis=dim)
        tail = lax.slice_in_dim(cells, cells.shape[dim] - width, cells.shape[dim], axis=dim)
        cells = jnp.concatenate(
            [
                lax.ppermute(tail, axis, [(i, (i + 1) % count) for i in range(ends)]),
                cells,
                lax.ppermute(head, axis, [((i + 1) % count, i) for i in range(ends)]),
            ],
            axis=dim,
        )
    return cells


def passed_along(value, axis, steps):
    count = lax.axis_size(axis)
    initial, last = (max(0, -steps), min(count, count - steps))
    return lax.ppermute(value, axis, [(source, source + steps) for source in range(initial, last)])


def shifted(array, offset):
    lead = array.ndim - 3
    sizes = array.shape[-3:]
    picks = tuple(
        (slice(1 + offset[axis_no], sizes[axis_no] - 1 + offset[axis_no]) for axis_no in range(3))
    )
    return array[(slice(None),) * lead + picks]


def grid_step(field_ext, kappa_ext, rate_mid):
    padded = jnp.pad(field_ext, ((0, 0), (0, 0), (1, 1), (1, 1)))
    kappa_pad = jnp.pad(kappa_ext, ((0, 0), (1, 1), (1, 1)))
    centre = padded[:, 1:-1, 1:-1, 1:-1]
    kappa_mid = kappa_pad[1:-1, 1:-1, 1:-1]
    change = jnp.zeros_like(centre)
    for offset in ((1, 0, 0), (-1, 0, 0), (0, 1, 0), (0, -1, 0), (0, 0, 1), (0, 0, -1)):
        change = change + 0.5 * (kappa_mid + shifted(kappa_pad, offset)) * (
            shifted(padded, offset) - centre
        )
    return centre + change + rate_mid * (centre - centre * centre * centre)


def deep_run(padded, kappa_ext, rate_ext, offset_rows, total_rows, slab_rows):
    for substep in range(3):
        extent = 3 - substep
        kappa_part = kappa_ext[3 - extent : 3 + slab_rows + extent]
        rate_part = rate_ext[4 - extent : 2 + slab_rows + extent]
        padded = grid_step(padded, kappa_part, rate_part)
        positions = offset_rows - (extent - 1) + jnp.arange(slab_rows + 2 * extent - 2)
        inside = ((positions >= 0) & (positions < total_rows)).astype(jnp.float32)
        padded = padded * inside[None, :, None, None]
    return padded


def pair_table(width):
    fine_index = jnp.arange(width)[:, None] // 2
    coarse_index = jnp.arange(width // 2)[None, :]
    return (fine_index == coarse_index).astype(jnp.float32)


def restrict(field_now):
    lead = field_now.shape[:-3]
    sizes = field_now.shape[-3:]
    blocks = field_now.reshape(lead + (sizes[0] // 2, 2, sizes[1] // 2, 2, sizes[2]))
    summed = jnp.sum(blocks, axis=(-4, -2))
    folded = jnp.matmul(summed, pair_table(sizes[2]), precision=lax.Precision.HIGHEST)
    return folded * 0.125


def prolong(coarse_field):
    width = coarse_field.shape[-1] * 2
    spread = jnp.matmul(coarse_field, pair_table(width).T, precision=lax.Precision.HIGHEST)
    return jnp.repeat(jnp.repeat(spread, 2, axis=-3), 2, axis=-2)


def shards(states, kappa, rate):
    slab_rows = kappa.shape[0]
    field_now = states
    kappa_ext, rate_ext = (
        extended_2(kappa, (("space", 0),), 1),
        extended_2(rate, (("space", 0),), 1),
    )
    for counter in range(STEPS):
        padded = extended_2(field_now, (("space", 1),), 1)
        field_now = grid_step(padded, kappa_ext, rate)
    coarse_rows = slab_rows // 2
    coarse_offset = lax.axis_index("space") * coarse_rows
    coarse_total = coarse_rows * lax.axis_size("space")
    kappa_small = restrict(kappa)
    rate_small = 4.0 * restrict(rate)
    kappa_wide, rate_wide = (
        extended_2(kappa_small, (("space", 0),), 3),
        extended_2(rate_small, (("space", 0),), 3),
    )

    def coarse_prop(coarse_field):
        extended = extended_2(coarse_field, (("space", 1),), 3)
        return deep_run(extended, kappa_wide, rate_wide, coarse_offset, coarse_total, coarse_rows)

    old_coarse = coarse_prop(restrict(states))
    deltas = restrict(field_now) - old_coarse
    carried = restrict(states[0:1])
    newer = jnp.zeros_like(old_coarse)
    group = lax.axis_index("tm")
    sections = lax.axis_size("tm")
    for section in range(sections):
        for window in range(states.shape[0]):
            moved = coarse_prop(carried)
            newer = newer.at[window].set(jnp.where(group == section, moved[0], newer[window]))
            carried = deltas[window : window + 1] + moved
        if section + 1 < sections:
            carried = passed_along(carried, "tm", 1)
    return field_now + prolong(newer - old_coarse)


def solution(mesh):
    in_specs = (P("tm", "space", None, None), P("space", None, None), P("space", None, None))
    out_specs = P("tm", "space", None, None)
    return jax.shard_map(shards, mesh=mesh, in_specs=in_specs, out_specs=out_specs, check_vma=False)
```

profile of v0, /device:TPU:26, one launch (start us, length us, event | category | flops | bytes accessed | tf_op | source)
XLA Modules:
  0.0 175.7 jit_solution(3283827158646414849)
XLA Ops:
  0.0 1.0 fusion.579
  1.0 2.8 %collective-permute-start.1 = (f32[2,1,64,128]{3,2,1,0:T(8,128)S(1)}, f32[2,1,64,128]{3,2,1,0:T(8,128)S(1)}, u32[]{:S(2)}, u32[]{:S(2)}) collective-permute-start(f32[2,1,64,128]{3,2,1,0:T(8,128)S(1)} %get-tuple-element.106), channel_id=1, source_target_pairs={{1,0},{2,1},{3,2},{4,3},{5,4},{6,5},{7,6},{8,7},{9,8},{10,9},{11,1... | collective-permute-start | bytes 196616 | tf_op jit(solution)/shard_map/ppermute | solution.py:19
  3.7 1.9 %collective-permute-start.3 = (f32[2,1,64,128]{3,2,1,0:T(8,128)S(1)}, f32[2,1,64,128]{3,2,1,0:T(8,128)S(1)}, u32[]{:S(2)}, u32[]{:S(2)}) collective-permute-start(f32[2,1,64,128]{3,2,1,0:T(8,128)S(1)} %get-tuple-element.105), channel_id=1, source_target_pairs={{0,1},{1,2},{2,3},{3,4},{4,5},{5,6},{6,7},{7,8},{8,9},{9,10},{10,1... | collective-permute-start | bytes 196616 | tf_op jit(solution)/shard_map/ppermute | solution.py:17
  5.7 0.8 fusion.580
  6.4 4.5 %collective-permute-start = (f32[1,64,128]{2,1,0:T(8,128)S(1)}, f32[1,64,128]{2,1,0:T(8,128)S(1)}, u32[]{:S(2)}, u32[]{:S(2)}) collective-permute-start(f32[1,64,128]{2,1,0:T(8,128)S(1)} %get-tuple-element.110), channel_id=1, source_target_pairs={{1,0},{2,1},{3,2},{4,3},{5,4},{6,5},{7,6},{8,7},{9,8},{10,9},{11,1... | collective-permute-start | bytes 98312 | tf_op jit(solution)/shard_map/ppermute | solution.py:19
  11.0 1.9 %collective-permute-start.2 = (f32[1,64,128]{2,1,0:T(8,128)S(1)}, f32[1,64,128]{2,1,0:T(8,128)S(1)}, u32[]{:S(2)}, u32[]{:S(2)}) collective-permute-start(f32[1,64,128]{2,1,0:T(8,128)S(1)} %get-tuple-element.109), channel_id=1, source_target_pairs={{0,1},{1,2},{2,3},{3,4},{4,5},{5,6},{6,7},{7,8},{8,9},{9,10},{10,1... | collective-permute-start | bytes 98312 | tf_op jit(solution)/shard_map/ppermute | solution.py:17
  12.9 1.5 reduce_sum.49
  14.6 4.5 %collective-permute-start.33 = (f32[2,3,32,64]{3,2,1,0:T(8,128)S(1)}, f32[2,3,32,64]{3,2,1,0:T(8,128)S(1)}, u32[]{:S(2)}, u32[]{:S(2)}) collective-permute-start(f32[2,3,32,64]{3,2,1,0:T(8,128)S(1)} %get-tuple-element.112), channel_id=1, source_target_pairs={{1,0},{2,1},{3,2},{4,3},{5,4},{6,5},{7,6},{8,7},{9,8},{10,9},{11,1... | collective-permute-start | bytes 147464 | tf_op jit(solution)/shard_map/ppermute | solution.py:19
  20.5 1.9 %collective-permute-start.32 = (f32[2,3,32,64]{3,2,1,0:T(8,128)S(1)}, f32[2,3,32,64]{3,2,1,0:T(8,128)S(1)}, u32[]{:S(2)}, u32[]{:S(2)}) collective-permute-start(f32[2,3,32,64]{3,2,1,0:T(8,128)S(1)} %get-tuple-element.111), channel_id=1, source_target_pairs={{0,1},{1,2},{2,3},{3,4},{4,5},{5,6},{6,7},{7,8},{8,9},{9,10},{10,1... | collective-permute-start | bytes 147464 | tf_op jit(solution)/shard_map/ppermute | solution.py:17
  22.4 4.5 %collective-permute-start.31 = (f32[3,32,64]{2,1,0:T(8,128)S(1)}, f32[3,32,64]{2,1,0:T(8,128)S(1)}, u32[]{:S(2)}, u32[]{:S(2)}) collective-permute-start(f32[3,32,64]{2,1,0:T(8,128)S(1)} %get-tuple-element.124), channel_id=1, source_target_pairs={{1,0},{2,1},{3,2},{4,3},{5,4},{6,5},{7,6},{8,7},{9,8},{10,9},{11,1... | collective-permute-start | bytes 73736 | tf_op jit(solution)/shard_map/ppermute | solution.py:19
  28.7 1.9 %collective-permute-start.4 = (f32[2,1,64,128]{3,2,1,0:T(8,128)S(1)}, f32[2,1,64,128]{3,2,1,0:T(8,128)S(1)}, u32[]{:S(2)}, u32[]{:S(2)}) collective-permute-start(f32[2,1,64,128]{3,2,1,0:T(8,128)S(1)} %get-tuple-element.104), channel_id=1, source_target_pairs={{1,0},{2,1},{3,2},{4,3},{5,4},{6,5},{7,6},{8,7},{9,8},{10,9},{11,1... | collective-permute-start | bytes 196616 | tf_op jit(solution)/shard_map/ppermute | solution.py:19
  30.6 2.4 %collective-permute-start.5 = (f32[2,1,64,128]{3,2,1,0:T(8,128)S(1)}, f32[2,1,64,128]{3,2,1,0:T(8,128)S(1)}, u32[]{:S(2)}, u32[]{:S(2)}) collective-permute-start(f32[2,1,64,128]{3,2,1,0:T(8,128)S(1)} %get-tuple-element.103), channel_id=1, source_target_pairs={{0,1},{1,2},{2,3},{3,4},{4,5},{5,6},{6,7},{7,8},{8,9},{9,10},{10,1... | collective-permute-start | bytes 196616 | tf_op jit(solution)/shard_map/ppermute | solution.py:17
  33.0 1.9 %collective-permute-start.30 = (f32[3,32,64]{2,1,0:T(8,128)S(1)}, f32[3,32,64]{2,1,0:T(8,128)S(1)}, u32[]{:S(2)}, u32[]{:S(2)}) collective-permute-start(f32[3,32,64]{2,1,0:T(8,128)S(1)} %get-tuple-element.123), channel_id=1, source_target_pairs={{0,1},{1,2},{2,3},{3,4},{4,5},{5,6},{6,7},{7,8},{8,9},{9,10},{10,1... | collective-permute-start | bytes 73736 | tf_op jit(solution)/shard_map/ppermute | solution.py:17
  34.9 2.1 %collective-permute-done.5 = f32[2,1,64,128]{3,2,1,0:T(8,128)S(1)} collective-permute-done((f32[2,1,64,128]{3,2,1,0:T(8,128)S(1)}, f32[2,1,64,128]{3,2,1,0:T(8,128)S(1)}, u32[]{:S(2)}, u32[]{:S(2)}) %collective-permute-start.5) | collective-permute-done | bytes 65568 | tf_op jit(solution)/shard_map/ppermute | solution.py:17
  37.1 2.4 %collective-permute-start.27 = (f32[1,3,32,64]{3,2,1,0:T(8,128)S(1)}, f32[1,3,32,64]{3,2,1,0:T(8,128)S(1)}, u32[]{:S(2)}, u32[]{:S(2)}) collective-permute-start(f32[1,3,32,64]{3,2,1,0:T(8,128)S(1)} %get-tuple-element.122), channel_id=1, source_target_pairs={{1,0},{2,1},{3,2},{4,3},{5,4},{6,5},{7,6},{8,7},{9,8},{10,9},{11,1... | collective-permute-start | bytes 73736 | tf_op jit(solution)/shard_map/ppermute | solution.py:19
  40.0 0.6 fusion.11
  40.6 1.9 %collective-permute-start.6 = (f32[2,1,64,128]{3,2,1,0:T(8,128)S(1)}, f32[2,1,64,128]{3,2,1,0:T(8,128)S(1)}, u32[]{:S(2)}, u32[]{:S(2)}) collective-permute-start(f32[2,1,64,128]{3,2,1,0:T(8,128)S(1)} %get-tuple-element.102), channel_id=1, source_target_pairs={{1,0},{2,1},{3,2},{4,3},{5,4},{6,5},{7,6},{8,7},{9,8},{10,9},{11,1... | collective-permute-start | bytes 196616 | tf_op jit(solution)/shard_map/ppermute | solution.py:19
  42.6 2.4 %collective-permute-start.7 = (f32[2,1,64,128]{3,2,1,0:T(8,128)S(1)}, f32[2,1,64,128]{3,2,1,0:T(8,128)S(1)}, u32[]{:S(2)}, u32[]{:S(2)}) collective-permute-start(f32[2,1,64,128]{3,2,1,0:T(8,128)S(1)} %get-tuple-element.101), channel_id=1, source_target_pairs={{0,1},{1,2},{2,3},{3,4},{4,5},{5,6},{6,7},{7,8},{8,9},{9,10},{10,1... | collective-permute-start | bytes 196616 | tf_op jit(solution)/shard_map/ppermute | solution.py:17
  45.0 3.1 %collective-permute-start.26 = (f32[1,3,32,64]{3,2,1,0:T(8,128)S(1)}, f32[1,3,32,64]{3,2,1,0:T(8,128)S(1)}, u32[]{:S(2)}, u32[]{:S(2)}) collective-permute-start(f32[1,3,32,64]{3,2,1,0:T(8,128)S(1)} %get-tuple-element.121), channel_id=1, source_target_pairs={{0,1},{1,2},{2,3},{3,4},{4,5},{5,6},{6,7},{7,8},{8,9},{9,10},{10,1... | collective-permute-start | bytes 73736 | tf_op jit(solution)/shard_map/ppermute | solution.py:17
  48.1 0.9 collective-permute-done.7
  49.1 2.5 %collective-permute-start.29 = (f32[3,32,64]{2,1,0:T(8,128)S(1)}, f32[3,32,64]{2,1,0:T(8,128)S(1)}, u32[]{:S(2)}, u32[]{:S(2)}) collective-permute-start(f32[3,32,64]{2,1,0:T(8,128)S(1)} %get-tuple-element.120), channel_id=1, source_target_pairs={{1,0},{2,1},{3,2},{4,3},{5,4},{6,5},{7,6},{8,7},{9,8},{10,9},{11,1... | collective-permute-start | bytes 73736 | tf_op jit(solution)/shard_map/ppermute | solution.py:19
  52.6 2.0 %collective-permute-start.8 = (f32[2,1,64,128]{3,2,1,0:T(8,128)S(1)}, f32[2,1,64,128]{3,2,1,0:T(8,128)S(1)}, u32[]{:S(2)}, u32[]{:S(2)}) collective-permute-start(f32[2,1,64,128]{3,2,1,0:T(8,128)S(1)} %get-tuple-element.100), channel_id=1, source_target_pairs={{1,0},{2,1},{3,2},{4,3},{5,4},{6,5},{7,6},{8,7},{9,8},{10,9},{11,1... | collective-permute-start | bytes 196616 | tf_op jit(solution)/shard_map/ppermute | solution.py:19
  54.7 2.3 %collective-permute-start.9 = (f32[2,1,64,128]{3,2,1,0:T(8,128)S(1)}, f32[2,1,64,128]{3,2,1,0:T(8,128)S(1)}, u32[]{:S(2)}, u32[]{:S(2)}) collective-permute-start(f32[2,1,64,128]{3,2,1,0:T(8,128)S(1)} %get-tuple-element.99), channel_id=1, source_target_pairs={{0,1},{1,2},{2,3},{3,4},{4,5},{5,6},{6,7},{7,8},{8,9},{9,10},{10,1... | collective-permute-start | bytes 196616 | tf_op jit(solution)/shard_map/ppermute | solution.py:17
  57.0 3.1 %collective-permute-start.28 = (f32[3,32,64]{2,1,0:T(8,128)S(1)}, f32[3,32,64]{2,1,0:T(8,128)S(1)}, u32[]{:S(2)}, u32[]{:S(2)}) collective-permute-start(f32[3,32,64]{2,1,0:T(8,128)S(1)} %get-tuple-element.119), channel_id=1, source_target_pairs={{0,1},{1,2},{2,3},{3,4},{4,5},{5,6},{6,7},{7,8},{8,9},{9,10},{10,1... | collective-permute-start | bytes 73736 | tf_op jit(solution)/shard_map/ppermute | solution.py:17
  60.1 1.1 collective-permute-done.9
  62.3 2.3 %collective-permute-start.10 = (f32[2,1,64,128]{3,2,1,0:T(8,128)S(1)}, f32[2,1,64,128]{3,2,1,0:T(8,128)S(1)}, u32[]{:S(2)}, u32[]{:S(2)}) collective-permute-start(f32[2,1,64,128]{3,2,1,0:T(8,128)S(1)} %get-tuple-element.98), channel_id=1, source_target_pairs={{1,0},{2,1},{3,2},{4,3},{5,4},{6,5},{7,6},{8,7},{9,8},{10,9},{11,1... | collective-permute-start | bytes 196616 | tf_op jit(solution)/shard_map/ppermute | solution.py:19
  64.6 2.0 %collective-permute-start.11 = (f32[2,1,64,128]{3,2,1,0:T(8,128)S(1)}, f32[2,1,64,128]{3,2,1,0:T(8,128)S(1)}, u32[]{:S(2)}, u32[]{:S(2)}) collective-permute-start(f32[2,1,64,128]{3,2,1,0:T(8,128)S(1)} %get-tuple-element.97), channel_id=1, source_target_pairs={{0,1},{1,2},{2,3},{3,4},{4,5},{5,6},{6,7},{7,8},{8,9},{9,10},{10,1... | collective-permute-start | bytes 196616 | tf_op jit(solution)/shard_map/ppermute | solution.py:17
  66.7 4.4 %collective-permute-done.11 = f32[2,1,64,128]{3,2,1,0:T(8,128)S(1)} collective-permute-done((f32[2,1,64,128]{3,2,1,0:T(8,128)S(1)}, f32[2,1,64,128]{3,2,1,0:T(8,128)S(1)}, u32[]{:S(2)}, u32[]{:S(2)}) %collective-permute-start.11) | collective-permute-done | bytes 65568 | tf_op jit(solution)/shard_map/ppermute | solution.py:17
  72.2 1.9 %collective-permute-start.12 = (f32[2,1,64,128]{3,2,1,0:T(8,128)S(1)}, f32[2,1,64,128]{3,2,1,0:T(8,128)S(1)}, u32[]{:S(2)}, u32[]{:S(2)}) collective-permute-start(f32[2,1,64,128]{3,2,1,0:T(8,128)S(1)} %get-tuple-element.96), channel_id=1, source_target_pairs={{1,0},{2,1},{3,2},{4,3},{5,4},{6,5},{7,6},{8,7},{9,8},{10,9},{11,1... | collective-permute-start | bytes 196616 | tf_op jit(solution)/shard_map/ppermute | solution.py:19
  74.2 2.4 %collective-permute-start.13 = (f32[2,1,64,128]{3,2,1,0:T(8,128)S(1)}, f32[2,1,64,128]{3,2,1,0:T(8,128)S(1)}, u32[]{:S(2)}, u32[]{:S(2)}) collective-permute-start(f32[2,1,64,128]{3,2,1,0:T(8,128)S(1)} %get-tuple-element.95), channel_id=1, source_target_pairs={{0,1},{1,2},{2,3},{3,4},{4,5},{5,6},{6,7},{7,8},{8,9},{9,10},{10,1... | collective-permute-start | bytes 196616 | tf_op jit(solution)/shard_map/ppermute | solution.py:17
  76.9 3.8 %collective-permute-done.13 = f32[2,1,64,128]{3,2,1,0:T(8,128)S(1)} collective-permute-done((f32[2,1,64,128]{3,2,1,0:T(8,128)S(1)}, f32[2,1,64,128]{3,2,1,0:T(8,128)S(1)}, u32[]{:S(2)}, u32[]{:S(2)}) %collective-permute-start.13) | collective-permute-done | bytes 65568 | tf_op jit(solution)/shard_map/ppermute | solution.py:17
  81.1 0.6 fusion.19
  81.8 1.9 %collective-permute-start.14 = (f32[2,1,64,128]{3,2,1,0:T(8,128)S(1)}, f32[2,1,64,128]{3,2,1,0:T(8,128)S(1)}, u32[]{:S(2)}, u32[]{:S(2)}) collective-permute-start(f32[2,1,64,128]{3,2,1,0:T(8,128)S(1)} %get-tuple-element.94), channel_id=1, source_target_pairs={{1,0},{2,1},{3,2},{4,3},{5,4},{6,5},{7,6},{8,7},{9,8},{10,9},{11,1... | collective-permute-start | bytes 196616 | tf_op jit(solution)/shard_map/ppermute | solution.py:19
  83.7 2.6 %collective-permute-start.15 = (f32[2,1,64,128]{3,2,1,0:T(8,128)S(1)}, f32[2,1,64,128]{3,2,1,0:T(8,128)S(1)}, u32[]{:S(2)}, u32[]{:S(2)}) collective-permute-start(f32[2,1,64,128]{3,2,1,0:T(8,128)S(1)} %get-tuple-element.93), channel_id=1, source_target_pairs={{0,1},{1,2},{2,3},{3,4},{4,5},{5,6},{6,7},{7,8},{8,9},{9,10},{10,1... | collective-permute-start | bytes 196616 | tf_op jit(solution)/shard_map/ppermute | solution.py:17
  86.5 3.7 %collective-permute-done.15 = f32[2,1,64,128]{3,2,1,0:T(8,128)S(1)} collective-permute-done((f32[2,1,64,128]{3,2,1,0:T(8,128)S(1)}, f32[2,1,64,128]{3,2,1,0:T(8,128)S(1)}, u32[]{:S(2)}, u32[]{:S(2)}) %collective-permute-start.15) | collective-permute-done | bytes 65568 | tf_op jit(solution)/shard_map/ppermute | solution.py:17
  91.3 1.9 %collective-permute-start.16 = (f32[2,1,64,128]{3,2,1,0:T(8,128)S(1)}, f32[2,1,64,128]{3,2,1,0:T(8,128)S(1)}, u32[]{:S(2)}, u32[]{:S(2)}) collective-permute-start(f32[2,1,64,128]{3,2,1,0:T(8,128)S(1)} %get-tuple-element.92), channel_id=1, source_target_pairs={{1,0},{2,1},{3,2},{4,3},{5,4},{6,5},{7,6},{8,7},{9,8},{10,9},{11,1... | collective-permute-start | bytes 196616 | tf_op jit(solution)/shard_map/ppermute | solution.py:19
  93.2 2.4 %collective-permute-start.17 = (f32[2,1,64,128]{3,2,1,0:T(8,128)S(1)}, f32[2,1,64,128]{3,2,1,0:T(8,128)S(1)}, u32[]{:S(2)}, u32[]{:S(2)}) collective-permute-start(f32[2,1,64,128]{3,2,1,0:T(8,128)S(1)} %get-tuple-element.91), channel_id=1, source_target_pairs={{0,1},{1,2},{2,3},{3,4},{4,5},{5,6},{6,7},{7,8},{8,9},{9,10},{10,1... | collective-permute-start | bytes 196616 | tf_op jit(solution)/shard_map/ppermute | solution.py:17
  95.8 3.9 %collective-permute-done.17 = f32[2,1,64,128]{3,2,1,0:T(8,128)S(1)} collective-permute-done((f32[2,1,64,128]{3,2,1,0:T(8,128)S(1)}, f32[2,1,64,128]{3,2,1,0:T(8,128)S(1)}, u32[]{:S(2)}, u32[]{:S(2)}) %collective-permute-start.17) | collective-permute-done | bytes 65568 | tf_op jit(solution)/shard_map/ppermute | solution.py:17
  100.2 0.6 fusion.23
  100.8 1.9 %collective-permute-start.18 = (f32[2,1,64,128]{3,2,1,0:T(8,128)S(1)}, f32[2,1,64,128]{3,2,1,0:T(8,128)S(1)}, u32[]{:S(2)}, u32[]{:S(2)}) collective-permute-start(f32[2,1,64,128]{3,2,1,0:T(8,128)S(1)} %get-tuple-element.90), channel_id=1, source_target_pairs={{1,0},{2,1},{3,2},{4,3},{5,4},{6,5},{7,6},{8,7},{9,8},{10,9},{11,1... | collective-permute-start | bytes 196616 | tf_op jit(solution)/shard_map/ppermute | solution.py:19
  102.8 2.4 %collective-permute-start.19 = (f32[2,1,64,128]{3,2,1,0:T(8,128)S(1)}, f32[2,1,64,128]{3,2,1,0:T(8,128)S(1)}, u32[]{:S(2)}, u32[]{:S(2)}) collective-permute-start(f32[2,1,64,128]{3,2,1,0:T(8,128)S(1)} %get-tuple-element.89), channel_id=1, source_target_pairs={{0,1},{1,2},{2,3},{3,4},{4,5},{5,6},{6,7},{7,8},{8,9},{9,10},{10,1... | collective-permute-start | bytes 196616 | tf_op jit(solution)/shard_map/ppermute | solution.py:17
  105.2 4.0 %collective-permute-done.19 = f32[2,1,64,128]{3,2,1,0:T(8,128)S(1)} collective-permute-done((f32[2,1,64,128]{3,2,1,0:T(8,128)S(1)}, f32[2,1,64,128]{3,2,1,0:T(8,128)S(1)}, u32[]{:S(2)}, u32[]{:S(2)}) %collective-permute-start.19) | collective-permute-done | bytes 65568 | tf_op jit(solution)/shard_map/ppermute | solution.py:17
  109.7 0.6 fusion.25
  110.4 1.9 %collective-permute-start.20 = (f32[2,1,64,128]{3,2,1,0:T(8,128)S(1)}, f32[2,1,64,128]{3,2,1,0:T(8,128)S(1)}, u32[]{:S(2)}, u32[]{:S(2)}) collective-permute-start(f32[2,1,64,128]{3,2,1,0:T(8,128)S(1)} %get-tuple-element.88), channel_id=1, source_target_pairs={{1,0},{2,1},{3,2},{4,3},{5,4},{6,5},{7,6},{8,7},{9,8},{10,9},{11,1... | collective-permute-start | bytes 196616 | tf_op jit(solution)/shard_map/ppermute | solution.py:19
  112.3 2.4 %collective-permute-start.21 = (f32[2,1,64,128]{3,2,1,0:T(8,128)S(1)}, f32[2,1,64,128]{3,2,1,0:T(8,128)S(1)}, u32[]{:S(2)}, u32[]{:S(2)}) collective-permute-start(f32[2,1,64,128]{3,2,1,0:T(8,128)S(1)} %get-tuple-element.87), channel_id=1, source_target_pairs={{0,1},{1,2},{2,3},{3,4},{4,5},{5,6},{6,7},{7,8},{8,9},{9,10},{10,1... | collective-permute-start | bytes 196616 | tf_op jit(solution)/shard_map/ppermute | solution.py:17
  115.0 3.7 %collective-permute-done.21 = f32[2,1,64,128]{3,2,1,0:T(8,128)S(1)} collective-permute-done((f32[2,1,64,128]{3,2,1,0:T(8,128)S(1)}, f32[2,1,64,128]{3,2,1,0:T(8,128)S(1)}, u32[]{:S(2)}, u32[]{:S(2)}) %collective-permute-start.21) | collective-permute-done | bytes 65568 | tf_op jit(solution)/shard_map/ppermute | solution.py:17
  119.9 1.9 %collective-permute-start.22 = (f32[2,1,64,128]{3,2,1,0:T(8,128)S(1)}, f32[2,1,64,128]{3,2,1,0:T(8,128)S(1)}, u32[]{:S(2)}, u32[]{:S(2)}) collective-permute-start(f32[2,1,64,128]{3,2,1,0:T(8,128)S(1)} %get-tuple-element.86), channel_id=1, source_target_pairs={{1,0},{2,1},{3,2},{4,3},{5,4},{6,5},{7,6},{8,7},{9,8},{10,9},{11,1... | collective-permute-start | bytes 196616 | tf_op jit(solution)/shard_map/ppermute | solution.py:19
  121.8 2.4 %collective-permute-start.23 = (f32[2,1,64,128]{3,2,1,0:T(8,128)S(1)}, f32[2,1,64,128]{3,2,1,0:T(8,128)S(1)}, u32[]{:S(2)}, u32[]{:S(2)}) collective-permute-start(f32[2,1,64,128]{3,2,1,0:T(8,128)S(1)} %get-tuple-element.85), channel_id=1, source_target_pairs={{0,1},{1,2},{2,3},{3,4},{4,5},{5,6},{6,7},{7,8},{8,9},{9,10},{10,1... | collective-permute-start | bytes 196616 | tf_op jit(solution)/shard_map/ppermute | solution.py:17
  124.5 3.8 %collective-permute-done.23 = f32[2,1,64,128]{3,2,1,0:T(8,128)S(1)} collective-permute-done((f32[2,1,64,128]{3,2,1,0:T(8,128)S(1)}, f32[2,1,64,128]{3,2,1,0:T(8,128)S(1)}, u32[]{:S(2)}, u32[]{:S(2)}) %collective-permute-start.23) | collective-permute-done | bytes 65568 | tf_op jit(solution)/shard_map/ppermute | solution.py:17
  129.4 1.9 %collective-permute-start.24 = (f32[2,1,64,128]{3,2,1,0:T(8,128)S(1)}, f32[2,1,64,128]{3,2,1,0:T(8,128)S(1)}, u32[]{:S(2)}, u32[]{:S(2)}) collective-permute-start(f32[2,1,64,128]{3,2,1,0:T(8,128)S(1)} %get-tuple-element.84), channel_id=1, source_target_pairs={{1,0},{2,1},{3,2},{4,3},{5,4},{6,5},{7,6},{8,7},{9,8},{10,9},{11,1... | collective-permute-start | bytes 196616 | tf_op jit(solution)/shard_map/ppermute | solution.py:19
  131.3 2.4 %collective-permute-start.25 = (f32[2,1,64,128]{3,2,1,0:T(8,128)S(1)}, f32[2,1,64,128]{3,2,1,0:T(8,128)S(1)}, u32[]{:S(2)}, u32[]{:S(2)}) collective-permute-start(f32[2,1,64,128]{3,2,1,0:T(8,128)S(1)} %get-tuple-element.83), channel_id=1, source_target_pairs={{0,1},{1,2},{2,3},{3,4},{4,5},{5,6},{6,7},{7,8},{8,9},{9,10},{10,1... | collective-permute-start | bytes 196616 | tf_op jit(solution)/shard_map/ppermute | solution.py:17
  133.9 3.9 %collective-permute-done.25 = f32[2,1,64,128]{3,2,1,0:T(8,128)S(1)} collective-permute-done((f32[2,1,64,128]{3,2,1,0:T(8,128)S(1)}, f32[2,1,64,128]{3,2,1,0:T(8,128)S(1)}, u32[]{:S(2)}, u32[]{:S(2)}) %collective-permute-start.25) | collective-permute-done | bytes 65568 | tf_op jit(solution)/shard_map/ppermute | solution.py:17
  139.6 1.9 %collective-permute-start.35 = (f32[1,3,32,64]{3,2,1,0:T(8,128)S(1)}, f32[1,3,32,64]{3,2,1,0:T(8,128)S(1)}, u32[]{:S(2)}, u32[]{:S(2)}) collective-permute-start(f32[1,3,32,64]{3,2,1,0:T(8,128)S(1)} %get-tuple-element.118), channel_id=1, source_target_pairs={{1,0},{2,1},{3,2},{4,3},{5,4},{6,5},{7,6},{8,7},{9,8},{10,9},{11,1... | collective-permute-start | bytes 73736 | tf_op jit(solution)/shard_map/ppermute | solution.py:19
  141.5 2.4 %collective-permute-start.34 = (f32[1,3,32,64]{3,2,1,0:T(8,128)S(1)}, f32[1,3,32,64]{3,2,1,0:T(8,128)S(1)}, u32[]{:S(2)}, u32[]{:S(2)}) collective-permute-start(f32[1,3,32,64]{3,2,1,0:T(8,128)S(1)} %get-tuple-element.117), channel_id=1, source_target_pairs={{0,1},{1,2},{2,3},{3,4},{4,5},{5,6},{6,7},{7,8},{8,9},{9,10},{10,1... | collective-permute-start | bytes 73736 | tf_op jit(solution)/shard_map/ppermute | solution.py:17
  143.9 3.9 %collective-permute-done.34 = f32[1,3,32,64]{3,2,1,0:T(8,128)S(1)} collective-permute-done((f32[1,3,32,64]{3,2,1,0:T(8,128)S(1)}, f32[1,3,32,64]{3,2,1,0:T(8,128)S(1)}, u32[]{:S(2)}, u32[]{:S(2)}) %collective-permute-start.34) | collective-permute-done | bytes 24608 | tf_op jit(solution)/shard_map/ppermute | solution.py:17
  148.3 1.3 collective-permute-start.36
  149.6 4.8 %collective-permute-done.36 = f32[1,4,32,64]{3,2,1,0:T(8,128)S(1)} collective-permute-done((f32[1,4,32,64]{3,2,1,0:T(8,128)S(1)}, f32[1,4,32,64]{3,2,1,0:T(8,128)S(1)}, u32[]{:S(2)}, u32[]{:S(2)}) %collective-permute-start.36) | collective-permute-done | bytes 32800 | tf_op jit(solution)/shard_map/ppermute | solution.py:29
  154.4 1.9 %collective-permute-start.37 = (f32[1,3,32,64]{3,2,1,0:T(8,128)S(1)}, f32[1,3,32,64]{3,2,1,0:T(8,128)S(1)}, u32[]{:S(2)}, u32[]{:S(2)}) collective-permute-start(f32[1,3,32,64]{3,2,1,0:T(8,128)S(1)} %get-tuple-element.116), channel_id=1, source_target_pairs={{0,1},{1,2},{2,3},{3,4},{4,5},{5,6},{6,7},{7,8},{8,9},{9,10},{10,1... | collective-permute-start | bytes 73736 | tf_op jit(solution)/shard_map/ppermute | solution.py:17
  156.4 4.5 %collective-permute-start.38 = (f32[1,3,32,64]{3,2,1,0:T(8,128)S(1)}, f32[1,3,32,64]{3,2,1,0:T(8,128)S(1)}, u32[]{:S(2)}, u32[]{:S(2)}) collective-permute-start(f32[1,3,32,64]{3,2,1,0:T(8,128)S(1)} %get-tuple-element.115), channel_id=1, source_target_pairs={{1,0},{2,1},{3,2},{4,3},{5,4},{6,5},{7,6},{8,7},{9,8},{10,9},{11,1... | collective-permute-start | bytes 73736 | tf_op jit(solution)/shard_map/ppermute | solution.py:19
  161.0 1.7 collective-permute-done.38
  163.1 4.6 %collective-permute-start.40 = (f32[1,3,32,64]{3,2,1,0:T(8,128)S(1)}, f32[1,3,32,64]{3,2,1,0:T(8,128)S(1)}, u32[]{:S(2)}, u32[]{:S(2)}) collective-permute-start(f32[1,3,32,64]{3,2,1,0:T(8,128)S(1)} %get-tuple-element.114), channel_id=1, source_target_pairs={{1,0},{2,1},{3,2},{4,3},{5,4},{6,5},{7,6},{8,7},{9,8},{10,9},{11,1... | collective-permute-start | bytes 73736 | tf_op jit(solution)/shard_map/ppermute | solution.py:19
  167.7 1.9 %collective-permute-start.39 = (f32[1,3,32,64]{3,2,1,0:T(8,128)S(1)}, f32[1,3,32,64]{3,2,1,0:T(8,128)S(1)}, u32[]{:S(2)}, u32[]{:S(2)}) collective-permute-start(f32[1,3,32,64]{3,2,1,0:T(8,128)S(1)} %get-tuple-element.113), channel_id=1, source_target_pairs={{0,1},{1,2},{2,3},{3,4},{4,5},{5,6},{6,7},{7,8},{8,9},{9,10},{10,1... | collective-permute-start | bytes 73736 | tf_op jit(solution)/shard_map/ppermute | solution.py:17
  169.7 4.3 %collective-permute-done.39 = f32[1,3,32,64]{3,2,1,0:T(8,128)S(1)} collective-permute-done((f32[1,3,32,64]{3,2,1,0:T(8,128)S(1)}, f32[1,3,32,64]{3,2,1,0:T(8,128)S(1)}, u32[]{:S(2)}, u32[]{:S(2)}) %collective-permute-start.39) | collective-permute-done | bytes 24608 | tf_op jit(solution)/shard_map/ppermute | solution.py:17
  174.9 0.9 add.1137
  (133 shorter events, 16.3 us)
Async XLA Ops:
  0.0 19.2 %copy-start.3 = (f32[2,8,64,128]{3,2,1,0:T(8,128)S(1)}, f32[2,8,64,128]{3,2,1,0:T(8,128)}, u32[]{:S(2)}) copy-start(f32[2,8,64,128]{3,2,1,0:T(8,128)} %param.11) | copy-start | bytes 1572868
  0.0 19.2 %copy-start = (f32[8,64,128]{2,1,0:T(8,128)S(1)}, f32[8,64,128]{2,1,0:T(8,128)}, u32[]{:S(2)}) copy-start(f32[8,64,128]{2,1,0:T(8,128)} %param.13) | copy-start | bytes 786436
  1.0 26.6 %collective-permute-start.1 = (f32[2,1,64,128]{3,2,1,0:T(8,128)S(1)}, f32[2,1,64,128]{3,2,1,0:T(8,128)S(1)}, u32[]{:S(2)}, u32[]{:S(2)}) collective-permute-start(f32[2,1,64,128]{3,2,1,0:T(8,128)S(1)} %get-tuple-element.106), channel_id=1, source_target_pairs={{1,0},{2,1},{3,2},{4,3},{5,4},{6,5},{7,6},{8,7},{9,8},{10,9},{11,1... | collective-permute-start | bytes 196616 | tf_op jit(solution)/shard_map/ppermute | solution.py:19
  3.7 23.8 %collective-permute-start.3 = (f32[2,1,64,128]{3,2,1,0:T(8,128)S(1)}, f32[2,1,64,128]{3,2,1,0:T(8,128)S(1)}, u32[]{:S(2)}, u32[]{:S(2)}) collective-permute-start(f32[2,1,64,128]{3,2,1,0:T(8,128)S(1)} %get-tuple-element.105), channel_id=1, source_target_pairs={{0,1},{1,2},{2,3},{3,4},{4,5},{5,6},{6,7},{7,8},{8,9},{9,10},{10,1... | collective-permute-start | bytes 196616 | tf_op jit(solution)/shard_map/ppermute | solution.py:17
  6.4 14.0 %collective-permute-start = (f32[1,64,128]{2,1,0:T(8,128)S(1)}, f32[1,64,128]{2,1,0:T(8,128)S(1)}, u32[]{:S(2)}, u32[]{:S(2)}) collective-permute-start(f32[1,64,128]{2,1,0:T(8,128)S(1)} %get-tuple-element.110), channel_id=1, source_target_pairs={{1,0},{2,1},{3,2},{4,3},{5,4},{6,5},{7,6},{8,7},{9,8},{10,9},{11,1... | collective-permute-start | bytes 98312 | tf_op jit(solution)/shard_map/ppermute | solution.py:19
  11.0 11.4 %collective-permute-start.2 = (f32[1,64,128]{2,1,0:T(8,128)S(1)}, f32[1,64,128]{2,1,0:T(8,128)S(1)}, u32[]{:S(2)}, u32[]{:S(2)}) collective-permute-start(f32[1,64,128]{2,1,0:T(8,128)S(1)} %get-tuple-element.109), channel_id=1, source_target_pairs={{0,1},{1,2},{2,3},{3,4},{4,5},{5,6},{6,7},{7,8},{8,9},{9,10},{10,1... | collective-permute-start | bytes 98312 | tf_op jit(solution)/shard_map/ppermute | solution.py:17
  12.9 7.1 %copy-start.6 = (f32[8,64,128]{2,1,0:T(8,128)S(1)}, f32[8,64,128]{2,1,0:T(8,128)}, u32[]{:S(2)}) copy-start(f32[8,64,128]{2,1,0:T(8,128)} %param.12) | copy-start | bytes 786436
  14.6 90.5 %collective-permute-start.33 = (f32[2,3,32,64]{3,2,1,0:T(8,128)S(1)}, f32[2,3,32,64]{3,2,1,0:T(8,128)S(1)}, u32[]{:S(2)}, u32[]{:S(2)}) collective-permute-start(f32[2,3,32,64]{3,2,1,0:T(8,128)S(1)} %get-tuple-element.112), channel_id=1, source_target_pairs={{1,0},{2,1},{3,2},{4,3},{5,4},{6,5},{7,6},{8,7},{9,8},{10,9},{11,1... | collective-permute-start | bytes 147464 | tf_op jit(solution)/shard_map/ppermute | solution.py:19
  20.5 84.7 %collective-permute-start.32 = (f32[2,3,32,64]{3,2,1,0:T(8,128)S(1)}, f32[2,3,32,64]{3,2,1,0:T(8,128)S(1)}, u32[]{:S(2)}, u32[]{:S(2)}) collective-permute-start(f32[2,3,32,64]{3,2,1,0:T(8,128)S(1)} %get-tuple-element.111), channel_id=1, source_target_pairs={{0,1},{1,2},{2,3},{3,4},{4,5},{5,6},{6,7},{7,8},{8,9},{9,10},{10,1... | collective-permute-start | bytes 147464 | tf_op jit(solution)/shard_map/ppermute | solution.py:17
  22.4 18.2 %collective-permute-start.31 = (f32[3,32,64]{2,1,0:T(8,128)S(1)}, f32[3,32,64]{2,1,0:T(8,128)S(1)}, u32[]{:S(2)}, u32[]{:S(2)}) collective-permute-start(f32[3,32,64]{2,1,0:T(8,128)S(1)} %get-tuple-element.124), channel_id=1, source_target_pairs={{1,0},{2,1},{3,2},{4,3},{5,4},{6,5},{7,6},{8,7},{9,8},{10,9},{11,1... | collective-permute-start | bytes 73736 | tf_op jit(solution)/shard_map/ppermute | solution.py:19
  28.7 4.4 %collective-permute-start.4 = (f32[2,1,64,128]{3,2,1,0:T(8,128)S(1)}, f32[2,1,64,128]{3,2,1,0:T(8,128)S(1)}, u32[]{:S(2)}, u32[]{:S(2)}) collective-permute-start(f32[2,1,64,128]{3,2,1,0:T(8,128)S(1)} %get-tuple-element.104), channel_id=1, source_target_pairs={{1,0},{2,1},{3,2},{4,3},{5,4},{6,5},{7,6},{8,7},{9,8},{10,9},{11,1... | collective-permute-start | bytes 196616 | tf_op jit(solution)/shard_map/ppermute | solution.py:19
  30.6 6.5 %collective-permute-start.5 = (f32[2,1,64,128]{3,2,1,0:T(8,128)S(1)}, f32[2,1,64,128]{3,2,1,0:T(8,128)S(1)}, u32[]{:S(2)}, u32[]{:S(2)}) collective-permute-start(f32[2,1,64,128]{3,2,1,0:T(8,128)S(1)} %get-tuple-element.103), channel_id=1, source_target_pairs={{0,1},{1,2},{2,3},{3,4},{4,5},{5,6},{6,7},{7,8},{8,9},{9,10},{10,1... | collective-permute-start | bytes 196616 | tf_op jit(solution)/shard_map/ppermute | solution.py:17
  33.0 9.5 %collective-permute-start.30 = (f32[3,32,64]{2,1,0:T(8,128)S(1)}, f32[3,32,64]{2,1,0:T(8,128)S(1)}, u32[]{:S(2)}, u32[]{:S(2)}) collective-permute-start(f32[3,32,64]{2,1,0:T(8,128)S(1)} %get-tuple-element.123), channel_id=1, source_target_pairs={{0,1},{1,2},{2,3},{3,4},{4,5},{5,6},{6,7},{7,8},{8,9},{9,10},{10,1... | collective-permute-start | bytes 73736 | tf_op jit(solution)/shard_map/ppermute | solution.py:17
  37.1 15.6 %collective-permute-start.27 = (f32[1,3,32,64]{3,2,1,0:T(8,128)S(1)}, f32[1,3,32,64]{3,2,1,0:T(8,128)S(1)}, u32[]{:S(2)}, u32[]{:S(2)}) collective-permute-start(f32[1,3,32,64]{3,2,1,0:T(8,128)S(1)} %get-tuple-element.122), channel_id=1, source_target_pairs={{1,0},{2,1},{3,2},{4,3},{5,4},{6,5},{7,6},{8,7},{9,8},{10,9},{11,1... | collective-permute-start | bytes 73736 | tf_op jit(solution)/shard_map/ppermute | solution.py:19
  40.6 4.4 %collective-permute-start.6 = (f32[2,1,64,128]{3,2,1,0:T(8,128)S(1)}, f32[2,1,64,128]{3,2,1,0:T(8,128)S(1)}, u32[]{:S(2)}, u32[]{:S(2)}) collective-permute-start(f32[2,1,64,128]{3,2,1,0:T(8,128)S(1)} %get-tuple-element.102), channel_id=1, source_target_pairs={{1,0},{2,1},{3,2},{4,3},{5,4},{6,5},{7,6},{8,7},{9,8},{10,9},{11,1... | collective-permute-start | bytes 196616 | tf_op jit(solution)/shard_map/ppermute | solution.py:19
  42.6 6.5 %collective-permute-start.7 = (f32[2,1,64,128]{3,2,1,0:T(8,128)S(1)}, f32[2,1,64,128]{3,2,1,0:T(8,128)S(1)}, u32[]{:S(2)}, u32[]{:S(2)}) collective-permute-start(f32[2,1,64,128]{3,2,1,0:T(8,128)S(1)} %get-tuple-element.101), channel_id=1, source_target_pairs={{0,1},{1,2},{2,3},{3,4},{4,5},{5,6},{6,7},{7,8},{8,9},{9,10},{10,1... | collective-permute-start | bytes 196616 | tf_op jit(solution)/shard_map/ppermute | solution.py:17
  45.0 50.8 %copy-start.1 = (f32[10,32,64]{2,1,0:T(8,128)}, f32[10,32,64]{2,1,0:T(8,128)S(1)}, u32[]{:S(2)}) copy-start(f32[10,32,64]{2,1,0:T(8,128)S(1)} %pad_maximum_fusion.29) | copy-start | bytes 245764
  45.0 9.7 %collective-permute-start.26 = (f32[1,3,32,64]{3,2,1,0:T(8,128)S(1)}, f32[1,3,32,64]{3,2,1,0:T(8,128)S(1)}, u32[]{:S(2)}, u32[]{:S(2)}) collective-permute-start(f32[1,3,32,64]{3,2,1,0:T(8,128)S(1)} %get-tuple-element.121), channel_id=1, source_target_pairs={{0,1},{1,2},{2,3},{3,4},{4,5},{5,6},{6,7},{7,8},{8,9},{9,10},{10,1... | collective-permute-start | bytes 73736 | tf_op jit(solution)/shard_map/ppermute | solution.py:17
  49.1 15.6 %collective-permute-start.29 = (f32[3,32,64]{2,1,0:T(8,128)S(1)}, f32[3,32,64]{2,1,0:T(8,128)S(1)}, u32[]{:S(2)}, u32[]{:S(2)}) collective-permute-start(f32[3,32,64]{2,1,0:T(8,128)S(1)} %get-tuple-element.120), channel_id=1, source_target_pairs={{1,0},{2,1},{3,2},{4,3},{5,4},{6,5},{7,6},{8,7},{9,8},{10,9},{11,1... | collective-permute-start | bytes 73736 | tf_op jit(solution)/shard_map/ppermute | solution.py:19
  52.6 4.4 %collective-permute-start.8 = (f32[2,1,64,128]{3,2,1,0:T(8,128)S(1)}, f32[2,1,64,128]{3,2,1,0:T(8,128)S(1)}, u32[]{:S(2)}, u32[]{:S(2)}) collective-permute-start(f32[2,1,64,128]{3,2,1,0:T(8,128)S(1)} %get-tuple-element.100), channel_id=1, source_target_pairs={{1,0},{2,1},{3,2},{4,3},{5,4},{6,5},{7,6},{8,7},{9,8},{10,9},{11,1... | collective-permute-start | bytes 196616 | tf_op jit(solution)/shard_map/ppermute | solution.py:19
  54.7 6.5 %collective-permute-start.9 = (f32[2,1,64,128]{3,2,1,0:T(8,128)S(1)}, f32[2,1,64,128]{3,2,1,0:T(8,128)S(1)}, u32[]{:S(2)}, u32[]{:S(2)}) collective-permute-start(f32[2,1,64,128]{3,2,1,0:T(8,128)S(1)} %get-tuple-element.99), channel_id=1, source_target_pairs={{0,1},{1,2},{2,3},{3,4},{4,5},{5,6},{6,7},{7,8},{8,9},{9,10},{10,1... | collective-permute-start | bytes 196616 | tf_op jit(solution)/shard_map/ppermute | solution.py:17
  57.0 9.6 %collective-permute-start.28 = (f32[3,32,64]{2,1,0:T(8,128)S(1)}, f32[3,32,64]{2,1,0:T(8,128)S(1)}, u32[]{:S(2)}, u32[]{:S(2)}) collective-permute-start(f32[3,32,64]{2,1,0:T(8,128)S(1)} %get-tuple-element.119), channel_id=1, source_target_pairs={{0,1},{1,2},{2,3},{3,4},{4,5},{5,6},{6,7},{7,8},{8,9},{9,10},{10,1... | collective-permute-start | bytes 73736 | tf_op jit(solution)/shard_map/ppermute | solution.py:17
  62.3 4.4 %collective-permute-start.10 = (f32[2,1,64,128]{3,2,1,0:T(8,128)S(1)}, f32[2,1,64,128]{3,2,1,0:T(8,128)S(1)}, u32[]{:S(2)}, u32[]{:S(2)}) collective-permute-start(f32[2,1,64,128]{3,2,1,0:T(8,128)S(1)} %get-tuple-element.98), channel_id=1, source_target_pairs={{1,0},{2,1},{3,2},{4,3},{5,4},{6,5},{7,6},{8,7},{9,8},{10,9},{11,1... | collective-permute-start | bytes 196616 | tf_op jit(solution)/shard_map/ppermute | solution.py:19
  64.6 6.5 %collective-permute-start.11 = (f32[2,1,64,128]{3,2,1,0:T(8,128)S(1)}, f32[2,1,64,128]{3,2,1,0:T(8,128)S(1)}, u32[]{:S(2)}, u32[]{:S(2)}) collective-permute-start(f32[2,1,64,128]{3,2,1,0:T(8,128)S(1)} %get-tuple-element.97), channel_id=1, source_target_pairs={{0,1},{1,2},{2,3},{3,4},{4,5},{5,6},{6,7},{7,8},{8,9},{9,10},{10,1... | collective-permute-start | bytes 196616 | tf_op jit(solution)/shard_map/ppermute | solution.py:17
  66.7 10.2 %copy-start.4 = (f32[10,32,64]{2,1,0:T(8,128)}, f32[10,32,64]{2,1,0:T(8,128)S(1)}, u32[]{:S(2)}) copy-start(f32[10,32,64]{2,1,0:T(8,128)S(1)} %pad_maximum_fusion.28) | copy-start | bytes 245764
  72.2 4.6 %collective-permute-start.12 = (f32[2,1,64,128]{3,2,1,0:T(8,128)S(1)}, f32[2,1,64,128]{3,2,1,0:T(8,128)S(1)}, u32[]{:S(2)}, u32[]{:S(2)}) collective-permute-start(f32[2,1,64,128]{3,2,1,0:T(8,128)S(1)} %get-tuple-element.96), channel_id=1, source_target_pairs={{1,0},{2,1},{3,2},{4,3},{5,4},{6,5},{7,6},{8,7},{9,8},{10,9},{11,1... | collective-permute-start | bytes 196616 | tf_op jit(solution)/shard_map/ppermute | solution.py:19
  74.2 6.5 %collective-permute-start.13 = (f32[2,1,64,128]{3,2,1,0:T(8,128)S(1)}, f32[2,1,64,128]{3,2,1,0:T(8,128)S(1)}, u32[]{:S(2)}, u32[]{:S(2)}) collective-permute-start(f32[2,1,64,128]{3,2,1,0:T(8,128)S(1)} %get-tuple-element.95), channel_id=1, source_target_pairs={{0,1},{1,2},{2,3},{3,4},{4,5},{5,6},{6,7},{7,8},{8,9},{9,10},{10,1... | collective-permute-start | bytes 196616 | tf_op jit(solution)/shard_map/ppermute | solution.py:17
  81.1 5.2 %copy-start.5 = (f32[10,32,64]{2,1,0:T(8,128)S(1)}, f32[10,32,64]{2,1,0:T(8,128)}, u32[]{:S(2)}) copy-start(f32[10,32,64]{2,1,0:T(8,128)} %copy-done.4) | copy-start | bytes 245764
  81.1 5.2 %slice-start.2 = ((f32[10,32,64]{2,1,0:T(8,128)}), f32[8,32,64]{2,1,0:T(8,128)S(1)}, s32[]{:S(2)}) async-start(f32[10,32,64]{2,1,0:T(8,128)} %copy-done.4), calls=%async_computation.2 | async-start | bytes 262144 | tf_op jit(solution)/shard_map/slice | solution.py:45
  81.8 4.7 %collective-permute-start.14 = (f32[2,1,64,128]{3,2,1,0:T(8,128)S(1)}, f32[2,1,64,128]{3,2,1,0:T(8,128)S(1)}, u32[]{:S(2)}, u32[]{:S(2)}) collective-permute-start(f32[2,1,64,128]{3,2,1,0:T(8,128)S(1)} %get-tuple-element.94), channel_id=1, source_target_pairs={{1,0},{2,1},{3,2},{4,3},{5,4},{6,5},{7,6},{8,7},{9,8},{10,9},{11,1... | collective-permute-start | bytes 196616 | tf_op jit(solution)/shard_map/ppermute | solution.py:19
  83.7 6.5 %collective-permute-start.15 = (f32[2,1,64,128]{3,2,1,0:T(8,128)S(1)}, f32[2,1,64,128]{3,2,1,0:T(8,128)S(1)}, u32[]{:S(2)}, u32[]{:S(2)}) collective-permute-start(f32[2,1,64,128]{3,2,1,0:T(8,128)S(1)} %get-tuple-element.93), channel_id=1, source_target_pairs={{0,1},{1,2},{2,3},{3,4},{4,5},{5,6},{6,7},{7,8},{8,9},{9,10},{10,1... | collective-permute-start | bytes 196616 | tf_op jit(solution)/shard_map/ppermute | solution.py:17
  90.6 5.0 %slice-start.3 = ((f32[10,32,64]{2,1,0:T(8,128)}), f32[6,32,64]{2,1,0:T(8,128)S(1)}, s32[]{:S(2)}) async-start(f32[10,32,64]{2,1,0:T(8,128)} %copy-done.4), calls=%async_computation.3 | async-start | bytes 196608 | tf_op jit(solution)/shard_map/slice | solution.py:45
  91.3 4.5 %collective-permute-start.16 = (f32[2,1,64,128]{3,2,1,0:T(8,128)S(1)}, f32[2,1,64,128]{3,2,1,0:T(8,128)S(1)}, u32[]{:S(2)}, u32[]{:S(2)}) collective-permute-start(f32[2,1,64,128]{3,2,1,0:T(8,128)S(1)} %get-tuple-element.92), channel_id=1, source_target_pairs={{1,0},{2,1},{3,2},{4,3},{5,4},{6,5},{7,6},{8,7},{9,8},{10,9},{11,1... | collective-permute-start | bytes 196616 | tf_op jit(solution)/shard_map/ppermute | solution.py:19
  93.2 6.5 %collective-permute-start.17 = (f32[2,1,64,128]{3,2,1,0:T(8,128)S(1)}, f32[2,1,64,128]{3,2,1,0:T(8,128)S(1)}, u32[]{:S(2)}, u32[]{:S(2)}) collective-permute-start(f32[2,1,64,128]{3,2,1,0:T(8,128)S(1)} %get-tuple-element.91), channel_id=1, source_target_pairs={{0,1},{1,2},{2,3},{3,4},{4,5},{5,6},{6,7},{7,8},{8,9},{9,10},{10,1... | collective-permute-start | bytes 196616 | tf_op jit(solution)/shard_map/ppermute | solution.py:17
  100.8 4.4 %collective-permute-start.18 = (f32[2,1,64,128]{3,2,1,0:T(8,128)S(1)}, f32[2,1,64,128]{3,2,1,0:T(8,128)S(1)}, u32[]{:S(2)}, u32[]{:S(2)}) collective-permute-start(f32[2,1,64,128]{3,2,1,0:T(8,128)S(1)} %get-tuple-element.90), channel_id=1, source_target_pairs={{1,0},{2,1},{3,2},{4,3},{5,4},{6,5},{7,6},{8,7},{9,8},{10,9},{11,1... | collective-permute-start | bytes 196616 | tf_op jit(solution)/shard_map/ppermute | solution.py:19
  102.8 6.5 %collective-permute-start.19 = (f32[2,1,64,128]{3,2,1,0:T(8,128)S(1)}, f32[2,1,64,128]{3,2,1,0:T(8,128)S(1)}, u32[]{:S(2)}, u32[]{:S(2)}) collective-permute-start(f32[2,1,64,128]{3,2,1,0:T(8,128)S(1)} %get-tuple-element.89), channel_id=1, source_target_pairs={{0,1},{1,2},{2,3},{3,4},{4,5},{5,6},{6,7},{7,8},{8,9},{9,10},{10,1... | collective-permute-start | bytes 196616 | tf_op jit(solution)/shard_map/ppermute | solution.py:17
  109.7 5.0 %slice-start = ((f32[10,32,64]{2,1,0:T(8,128)}), f32[8,32,64]{2,1,0:T(8,128)S(1)}, s32[]{:S(2)}) async-start(f32[10,32,64]{2,1,0:T(8,128)} %copy-done.1), calls=%async_computation | async-start | bytes 262144 | tf_op jit(solution)/shard_map/slice | solution.py:58
  110.4 4.7 %collective-permute-start.20 = (f32[2,1,64,128]{3,2,1,0:T(8,128)S(1)}, f32[2,1,64,128]{3,2,1,0:T(8,128)S(1)}, u32[]{:S(2)}, u32[]{:S(2)}) collective-permute-start(f32[2,1,64,128]{3,2,1,0:T(8,128)S(1)} %get-tuple-element.88), channel_id=1, source_target_pairs={{1,0},{2,1},{3,2},{4,3},{5,4},{6,5},{7,6},{8,7},{9,8},{10,9},{11,1... | collective-permute-start | bytes 196616 | tf_op jit(solution)/shard_map/ppermute | solution.py:19
  112.3 6.5 %collective-permute-start.21 = (f32[2,1,64,128]{3,2,1,0:T(8,128)S(1)}, f32[2,1,64,128]{3,2,1,0:T(8,128)S(1)}, u32[]{:S(2)}, u32[]{:S(2)}) collective-permute-start(f32[2,1,64,128]{3,2,1,0:T(8,128)S(1)} %get-tuple-element.87), channel_id=1, source_target_pairs={{0,1},{1,2},{2,3},{3,4},{4,5},{5,6},{6,7},{7,8},{8,9},{9,10},{10,1... | collective-permute-start | bytes 196616 | tf_op jit(solution)/shard_map/ppermute | solution.py:17
  119.2 5.0 %slice-start.1 = ((f32[10,32,64]{2,1,0:T(8,128)}), f32[6,32,64]{2,1,0:T(8,128)S(1)}, s32[]{:S(2)}) async-start(f32[10,32,64]{2,1,0:T(8,128)} %copy-done.1), calls=%async_computation.1 | async-start | bytes 196608 | tf_op jit(solution)/shard_map/slice | solution.py:58
  119.9 4.6 %collective-permute-start.22 = (f32[2,1,64,128]{3,2,1,0:T(8,128)S(1)}, f32[2,1,64,128]{3,2,1,0:T(8,128)S(1)}, u32[]{:S(2)}, u32[]{:S(2)}) collective-permute-start(f32[2,1,64,128]{3,2,1,0:T(8,128)S(1)} %get-tuple-element.86), channel_id=1, source_target_pairs={{1,0},{2,1},{3,2},{4,3},{5,4},{6,5},{7,6},{8,7},{9,8},{10,9},{11,1... | collective-permute-start | bytes 196616 | tf_op jit(solution)/shard_map/ppermute | solution.py:19
  121.8 6.5 %collective-permute-start.23 = (f32[2,1,64,128]{3,2,1,0:T(8,128)S(1)}, f32[2,1,64,128]{3,2,1,0:T(8,128)S(1)}, u32[]{:S(2)}, u32[]{:S(2)}) collective-permute-start(f32[2,1,64,128]{3,2,1,0:T(8,128)S(1)} %get-tuple-element.85), channel_id=1, source_target_pairs={{0,1},{1,2},{2,3},{3,4},{4,5},{5,6},{6,7},{7,8},{8,9},{9,10},{10,1... | collective-permute-start | bytes 196616 | tf_op jit(solution)/shard_map/ppermute | solution.py:17
  129.4 4.5 %collective-permute-start.24 = (f32[2,1,64,128]{3,2,1,0:T(8,128)S(1)}, f32[2,1,64,128]{3,2,1,0:T(8,128)S(1)}, u32[]{:S(2)}, u32[]{:S(2)}) collective-permute-start(f32[2,1,64,128]{3,2,1,0:T(8,128)S(1)} %get-tuple-element.84), channel_id=1, source_target_pairs={{1,0},{2,1},{3,2},{4,3},{5,4},{6,5},{7,6},{8,7},{9,8},{10,9},{11,1... | collective-permute-start | bytes 196616 | tf_op jit(solution)/shard_map/ppermute | solution.py:19
  131.3 6.5 %collective-permute-start.25 = (f32[2,1,64,128]{3,2,1,0:T(8,128)S(1)}, f32[2,1,64,128]{3,2,1,0:T(8,128)S(1)}, u32[]{:S(2)}, u32[]{:S(2)}) collective-permute-start(f32[2,1,64,128]{3,2,1,0:T(8,128)S(1)} %get-tuple-element.83), channel_id=1, source_target_pairs={{0,1},{1,2},{2,3},{3,4},{4,5},{5,6},{6,7},{7,8},{8,9},{9,10},{10,1... | collective-permute-start | bytes 196616 | tf_op jit(solution)/shard_map/ppermute | solution.py:17
  138.9 8.9 %copy-start.2 = (f32[10,32,64]{2,1,0:T(8,128)S(1)}, f32[10,32,64]{2,1,0:T(8,128)}, u32[]{:S(2)}) copy-start(f32[10,32,64]{2,1,0:T(8,128)} %copy-done.1) | copy-start | bytes 245764
  139.6 4.3 %collective-permute-start.35 = (f32[1,3,32,64]{3,2,1,0:T(8,128)S(1)}, f32[1,3,32,64]{3,2,1,0:T(8,128)S(1)}, u32[]{:S(2)}, u32[]{:S(2)}) collective-permute-start(f32[1,3,32,64]{3,2,1,0:T(8,128)S(1)} %get-tuple-element.118), channel_id=1, source_target_pairs={{1,0},{2,1},{3,2},{4,3},{5,4},{6,5},{7,6},{8,7},{9,8},{10,9},{11,1... | collective-permute-start | bytes 73736 | tf_op jit(solution)/shard_map/ppermute | solution.py:19
  141.5 6.3 %collective-permute-start.34 = (f32[1,3,32,64]{3,2,1,0:T(8,128)S(1)}, f32[1,3,32,64]{3,2,1,0:T(8,128)S(1)}, u32[]{:S(2)}, u32[]{:S(2)}) collective-permute-start(f32[1,3,32,64]{3,2,1,0:T(8,128)S(1)} %get-tuple-element.117), channel_id=1, source_target_pairs={{0,1},{1,2},{2,3},{3,4},{4,5},{5,6},{6,7},{7,8},{8,9},{9,10},{10,1... | collective-permute-start | bytes 73736 | tf_op jit(solution)/shard_map/ppermute | solution.py:17
  148.3 6.2 %collective-permute-start.36 = (f32[1,4,32,64]{3,2,1,0:T(8,128)S(1)}, f32[1,4,32,64]{3,2,1,0:T(8,128)S(1)}, u32[]{:S(2)}, u32[]{:S(2)}) collective-permute-start(f32[1,4,32,64]{3,2,1,0:T(8,128)S(1)} %get-tuple-element.55), channel_id=1, source_target_pairs={{0,16},{1,17},{2,18},{3,19},{4,20},{5,21},{6,22},{7,23},{8,24},{9,... | collective-permute-start | bytes 98312 | tf_op jit(solution)/shard_map/ppermute | solution.py:29
  154.4 6.5 %collective-permute-start.37 = (f32[1,3,32,64]{3,2,1,0:T(8,128)S(1)}, f32[1,3,32,64]{3,2,1,0:T(8,128)S(1)}, u32[]{:S(2)}, u32[]{:S(2)}) collective-permute-start(f32[1,3,32,64]{3,2,1,0:T(8,128)S(1)} %get-tuple-element.116), channel_id=1, source_target_pairs={{0,1},{1,2},{2,3},{3,4},{4,5},{5,6},{6,7},{7,8},{8,9},{9,10},{10,1... | collective-permute-start | bytes 73736 | tf_op jit(solution)/shard_map/ppermute | solution.py:17
  156.4 6.3 %collective-permute-start.38 = (f32[1,3,32,64]{3,2,1,0:T(8,128)S(1)}, f32[1,3,32,64]{3,2,1,0:T(8,128)S(1)}, u32[]{:S(2)}, u32[]{:S(2)}) collective-permute-start(f32[1,3,32,64]{3,2,1,0:T(8,128)S(1)} %get-tuple-element.115), channel_id=1, source_target_pairs={{1,0},{2,1},{3,2},{4,3},{5,4},{6,5},{7,6},{8,7},{9,8},{10,9},{11,1... | collective-permute-start | bytes 73736 | tf_op jit(solution)/shard_map/ppermute | solution.py:19
  163.1 6.5 %collective-permute-start.40 = (f32[1,3,32,64]{3,2,1,0:T(8,128)S(1)}, f32[1,3,32,64]{3,2,1,0:T(8,128)S(1)}, u32[]{:S(2)}, u32[]{:S(2)}) collective-permute-start(f32[1,3,32,64]{3,2,1,0:T(8,128)S(1)} %get-tuple-element.114), channel_id=1, source_target_pairs={{1,0},{2,1},{3,2},{4,3},{5,4},{6,5},{7,6},{8,7},{9,8},{10,9},{11,1... | collective-permute-start | bytes 73736 | tf_op jit(solution)/shard_map/ppermute | solution.py:19
  167.7 6.3 %collective-permute-start.39 = (f32[1,3,32,64]{3,2,1,0:T(8,128)S(1)}, f32[1,3,32,64]{3,2,1,0:T(8,128)S(1)}, u32[]{:S(2)}, u32[]{:S(2)}) collective-permute-start(f32[1,3,32,64]{3,2,1,0:T(8,128)S(1)} %get-tuple-element.113), channel_id=1, source_target_pairs={{0,1},{1,2},{2,3},{3,4},{4,5},{5,6},{6,7},{7,8},{8,9},{9,10},{10,1... | collective-permute-start | bytes 73736 | tf_op jit(solution)/shard_map/ppermute | solution.py:17
where the time goes:
time: 177 us; the launch traced here: 176 us
  starting transfers between devices  101 us (57%)
  waiting for transfers between devices  50.1 us (28%)
  other arithmetic  19.4 us (11%)
  local copies, waits for them, and re-layouts  2.22 us (1%)
    ppermute x20, starting transfers between devices, extended_2(): lax.ppermute(head, axis, [((i + 1) % count, i) for i in range(ends)])  53.9 us
    ppermute x20, starting transfers between devices, extended_2(): lax.ppermute(tail, axis, [(i, (i + 1) % count) for i in range(ends)])  46.3 us
    ppermute x20, waiting for transfers between devices, extended_2(): lax.ppermute(tail, axis, [(i, (i + 1) % count) for i in range(ends)])  43.5 us
    add x12, other arithmetic, grid_step(): return centre + change + rate_mid * (centre - centre * centre * centre)  7.53 us
    concatenate x19, other arithmetic, extended_2(): jnp.concatenate([lax.ppermute(tail, axis, [(i, (i + 1) % count) for i in...  5.73 us
    ppermute x1, waiting for transfers between devices, passed_along(): lax.ppermute(value, axis, [(source, source + steps) for source in range(i...  4.84 us
  transfers between devices with their start and end apart: 41, of which 15 were waited for; matrix products, arithmetic and copies ran while one was open for 8% of the time, Pallas kernels for 0%

commit v1 on v0

v1 whole, which is shorter than its diff:
```python
import functools

import jax
import jax.numpy as jnp
from jax import lax
from jax.experimental import pallas as pl
from jax.experimental.pallas import tpu as pltpu
from jax.sharding import PartitionSpec as P

STEPS = 12
COARSE = 3
DEPTH = 2
ROUNDS = STEPS // DEPTH
MESH = pl.DeviceIdType.MESH
A, R, XP, XM, YP, YM, ZP, ZM = range(8)


def y_next(plane):
    rows = plane.shape[0]
    return jnp.concatenate([plane[8:rows], pltpu.roll(plane[0:8], 7, 0)], axis=0)


def y_prev(plane):
    rows = plane.shape[0]
    return jnp.concatenate([pltpu.roll(plane[rows - 8 : rows], 1, 0), plane[0 : rows - 8]], axis=0)


def z_next(plane, stride):
    return pltpu.roll(plane, plane.shape[1] - stride, 1)


def z_prev(plane, stride):
    return pltpu.roll(plane, stride, 1)


def edge_masks(rows, lanes, stride):
    row = lax.broadcasted_iota(jnp.int32, (rows, lanes), 0)
    lane = lax.broadcasted_iota(jnp.int32, (rows, lanes), 1)
    return (
        jnp.where(row == rows - 1, 0.0, 1.0),
        jnp.where(row == 0, 0.0, 1.0),
        jnp.where(lane >= lanes - stride, 0.0, 1.0),
        jnp.where(lane < stride, 0.0, 1.0),
    )


def make_coefs(coef, field, reaction, low, high, stride, row_valid):
    rows, lanes = field.shape[-2:]
    y_up, y_down, z_up, z_down = edge_masks(rows, lanes, stride)

    def body(i, _):
        k = field[i]
        r = reaction[i]
        valid = row_valid(i)
        xp = 0.5 * (k + field[i + 1])
        xm = 0.5 * (k + field[i - 1])
        yp = 0.5 * (k + y_next(k) * y_up)
        ym = 0.5 * (k + y_prev(k) * y_down)
        zp = 0.5 * (k + z_next(k, stride) * z_up)
        zm = 0.5 * (k + z_prev(k, stride) * z_down)
        coef[A, i] = (1.0 + r - ((xp + xm) + (yp + ym) + (zp + zm))) * valid
        coef[R, i] = r * valid
        coef[XP, i] = xp * valid
        coef[XM, i] = xm * valid
        coef[YP, i] = yp * y_up * valid
        coef[YM, i] = ym * y_down * valid
        coef[ZP, i] = zp * z_up * valid
        coef[ZM, i] = zm * z_down * valid
        return 0

    lax.fori_loop(low, high, body, 0)


def grid_step(source, target, coef, low, high, stride):
    def body(i, _):
        u = source[i]
        total = u * (coef[A, i] - coef[R, i] * (u * u))
        total = total + (coef[XP, i] * source[i + 1] + coef[XM, i] * source[i - 1])
        total = total + (coef[YP, i] * y_next(u) + coef[YM, i] * y_prev(u))
        total = total + (coef[ZP, i] * z_next(u, stride) + coef[ZM, i] * z_prev(u, stride))
        target[i] = total
        return 0

    lax.fori_loop(low, high, body, 0)


def restrict_rows(first, second):
    both = first + second
    rows, lanes = both.shape
    pairs = jnp.concatenate(
        [both[j : j + 8] + both[j + 8 : j + 16] for j in range(0, rows, 16)], axis=0
    )
    lane = lax.broadcasted_iota(jnp.int32, pairs.shape, 1)
    other = jnp.where(lane % 2 == 0, z_next(pairs, 1), z_prev(pairs, 1))
    return (pairs + other) * 0.125


def prolong_rows(plane):
    rows = plane.shape[0]
    return jnp.concatenate(
        [plane[j : j + 8] for j in range(0, rows, 8) for _ in range(2)], axis=0
    )


def kernel(
    count, groups, states, kappa, rate, out,
    u, temp, raw_u, raw_k, raw_r, kx, rx, coef,
    kc, rc, ccoef, ctemp, cstate, old, chain, newer, passed, outgoing,
    send, recv, tm_send, tm_recv,
):
    windows, n, rows, lanes = states.shape
    ext = n + 2 * DEPTH
    nc = n // 2
    side = COARSE
    cext = nc + 2 * side
    per = rows // 8
    rate_rows = max(DEPTH - 1, 1)
    me = lax.axis_index("space")
    group = lax.axis_index("tm")
    left = lax.rem(me + count - 1, count)
    right = lax.rem(me + 1, count)
    has_left = me > 0
    has_right = me < count - 1

    def when_left(fn):
        pl.when(has_left)(fn)

    def when_right(fn):
        pl.when(has_right)(fn)

    class Swap:
        def __init__(self, head, tail, left_halo, right_halo, slot):
            self.to_left = pltpu.make_async_remote_copy(
                src_ref=head, dst_ref=right_halo, send_sem=send.at[slot, 0],
                recv_sem=recv.at[slot, 1], device_id={"space": left}, device_id_type=MESH,
            )
            self.to_right = pltpu.make_async_remote_copy(
                src_ref=tail, dst_ref=left_halo, send_sem=send.at[slot, 1],
                recv_sem=recv.at[slot, 0], device_id={"space": right}, device_id_type=MESH,
            )

        def start(self):
            when_left(self.to_left.start)
            when_right(self.to_right.start)

        def arrived(self):
            when_left(self.to_right.wait_recv)
            when_right(self.to_left.wait_recv)

        def sent(self):
            when_left(self.to_left.wait_send)
            when_right(self.to_right.wait_send)

    def padded_swap(ref, width, depth, slot):
        return Swap(
            ref.at[pl.ds(depth, depth)], ref.at[pl.ds(width, depth)],
            ref.at[pl.ds(0, depth)], ref.at[pl.ds(width + depth, depth)], slot,
        )

    slot_k, slot_r, slot_kc, slot_rc = (windows + i for i in range(4))
    slot_old = windows + 4
    slot_chain = 2 * windows + 4
    slot_round = 3 * windows + 4

    def raw_swap(source, target, depth, slot):
        return Swap(
            source.at[pl.ds(0, depth)], source.at[pl.ds(n - depth, depth)],
            target.at[0], target.at[1], slot,
        )

    first_u = [raw_swap(states.at[w], raw_u.at[w], DEPTH, w) for w in range(windows)]
    first_k = raw_swap(kappa, raw_k, DEPTH, slot_k)
    first_r = raw_swap(rate, raw_r, rate_rows, slot_r)
    coarse_k = padded_swap(kc, nc, side, slot_kc)
    coarse_r = padded_swap(rc, nc, side, slot_rc)
    coarse_old = [padded_swap(cstate.at[w], nc, side, slot_old + w) for w in range(windows)]
    coarse_chain = [padded_swap(chain.at[w], nc, side, slot_chain + w) for w in range(windows)]

    def round_swap(r, w):
        return padded_swap(u.at[r, w], n, DEPTH, slot_round + r * windows + w)

    barrier = pltpu.get_barrier_semaphore()

    def greet(where):
        pl.semaphore_signal(barrier, inc=1, device_id=where, device_id_type=MESH)

    when_left(lambda: greet({"space": left}))
    when_right(lambda: greet({"space": right}))
    pl.when(group > 0)(lambda: greet({"tm": lax.rem(group + groups - 1, groups)}))
    pl.when(group < groups - 1)(lambda: greet({"tm": lax.rem(group + 1, groups)}))

    def load_plane(ref, *index):
        return jnp.concatenate(
            [ref[(*index, pl.ds(j, 8, stride=per), slice(None))] for j in range(per)], axis=0
        )

    def fill_own(i, _):
        kx[DEPTH + i] = load_plane(kappa, i)
        rx[DEPTH + i] = load_plane(rate, i)
        for w in range(windows):
            u[0, w, DEPTH + i] = load_plane(states, w, i)
        return 0

    lax.fori_loop(0, n, fill_own, 0)

    def zero(ref, low, size):
        ref[pl.ds(low, size)] = jnp.zeros((size,) + ref.shape[1:], jnp.float32)

    def zero_side(fine_low, coarse_low):
        zero(kx, fine_low, DEPTH)
        zero(rx, fine_low, DEPTH)
        zero(kc, coarse_low, side)
        zero(rc, coarse_low, side)
        for w in range(windows):
            zero(cstate.at[w], coarse_low, side)
            zero(chain.at[w], coarse_low, side)
            for r in range(ROUNDS):
                zero(u.at[r, w], fine_low, DEPTH)

    pl.when(me == 0)(lambda: zero_side(0, 0))
    pl.when(me == count - 1)(lambda: zero_side(n + DEPTH, nc + side))

    peers = [has_left, has_right, group > 0, group < groups - 1]
    pl.semaphore_wait(barrier, sum(jnp.where(there, 1, 0) for there in peers))

    first_k.start()
    first_r.start()
    for swap in first_u:
        swap.start()

    def coarse_rows(i, _):
        base = DEPTH + 2 * i
        kc[side + i] = restrict_rows(kx[base], kx[base + 1])
        rc[side + i] = 4.0 * restrict_rows(rx[base], rx[base + 1])
        for w in range(windows):
            cstate[w, side + i] = restrict_rows(u[0, w, base], u[0, w, base + 1])
        return 0

    lax.fori_loop(0, nc, coarse_rows, 0)
    coarse_k.start()
    coarse_r.start()
    for swap in coarse_old:
        swap.start()

    def fine_valid(i):
        place = me * n + i - DEPTH
        return jnp.where((place >= 0) & (place < count * n), 1.0, 0.0)

    def coarse_valid(i):
        place = me * nc + i - side
        return jnp.where((place >= 0) & (place < count * nc), 1.0, 0.0)

    make_coefs(coef, kx, rx, DEPTH + 1, DEPTH + n - 1, 1, fine_valid)

    first_k.arrived()
    first_r.arrived()

    def unpack_k(which, low, rate_low):
        for i in range(DEPTH):
            kx[low + i] = load_plane(raw_k, which, i)
        for i in range(rate_rows):
            rx[rate_low + i] = load_plane(raw_r, which, i)

    when_left(lambda: unpack_k(0, 0, DEPTH - rate_rows))
    when_right(lambda: unpack_k(1, n + DEPTH, n + DEPTH))
    make_coefs(coef, kx, rx, 1, DEPTH + 1, 1, fine_valid)
    make_coefs(coef, kx, rx, DEPTH + n - 1, ext - 1, 1, fine_valid)

    def fine_round(r, w):
        source = u.at[r, w]
        for k in range(1, DEPTH + 1):
            target = u.at[r + 1, w] if k == DEPTH else temp.at[k % 2]
            grid_step(source, target, coef, k, ext - k, 1)
            source = target

    def unpack_u(w, which, low):
        for i in range(DEPTH):
            u[0, w, low + i] = load_plane(raw_u, w, which, i)

    for w in range(windows):
        first_u[w].arrived()
        when_left(functools.partial(unpack_u, w, 0, 0))
        when_right(functools.partial(unpack_u, w, 1, n + DEPTH))
        fine_round(0, w)
        if ROUNDS > 1:
            round_swap(1, w).start()

    def coarse_run(source, target):
        for k in range(1, COARSE):
            dest = ctemp.at[k % 2]
            grid_step(source, dest, ccoef, k, cext - k, 2)
            source = dest
        grid_step(source, target, ccoef, COARSE, cext - COARSE, 2)

    coarse_k.arrived()
    coarse_r.arrived()
    make_coefs(ccoef, kc, rc, 1, cext - 1, 2, coarse_valid)
    for w in range(windows):
        coarse_old[w].arrived()
        coarse_run(cstate.at[w], old.at[w])

    def middle(r, _):
        for w in range(windows):
            round_swap(r, w).arrived()
            fine_round(r, w)
            round_swap(r + 1, w).start()
        return 0

    lax.fori_loop(1, ROUNDS - 1, middle, 0)

    def deltas(w, i):
        base = DEPTH + 2 * i
        ends = restrict_rows(u[ROUNDS, w, base], u[ROUNDS, w, base + 1])
        return (ends - old[w, side + i]) + newer[w, side + i]

    def carry_on(w):
        def body(i, _):
            chain[w + 1, side + i] = deltas(w, i)
            return 0

        lax.fori_loop(0, nc, body, 0)

    def take_old():
        newer[0, pl.ds(side, nc)] = old[0, pl.ds(side, nc)]

    incoming = pltpu.make_async_remote_copy(
        src_ref=outgoing, dst_ref=passed, send_sem=tm_send, recv_sem=tm_recv,
        device_id={"tm": lax.rem(group + 1, groups)}, device_id_type=MESH,
    ) if groups > 1 else None

    for w in range(windows):
        if ROUNDS > 1:
            round_swap(ROUNDS - 1, w).arrived()
            fine_round(ROUNDS - 1, w)
        if w == 0:
            pl.when(group == 0)(take_old)
            if windows > 1:
                def start_chain():
                    carry_on(0)
                    coarse_chain[1].start()

                pl.when(group == 0)(start_chain)

    if groups > 1:
        def from_before():
            incoming.wait_recv()
            chain[0, pl.ds(side, nc)] = passed[...]
            coarse_chain[0].start()
            coarse_chain[0].arrived()
            coarse_run(chain.at[0], newer.at[0])
            if windows > 1:
                carry_on(0)
                coarse_chain[1].start()

        pl.when(group > 0)(from_before)

    for w in range(1, windows):
        coarse_chain[w].arrived()
        coarse_run(chain.at[w], newer.at[w])
        if w + 1 < windows:
            carry_on(w)
            coarse_chain[w + 1].start()

    if groups > 1:
        def to_next():
            def body(i, _):
                outgoing[i] = deltas(windows - 1, i)
                return 0

            lax.fori_loop(0, nc, body, 0)
            incoming.start()

        pl.when(group < groups - 1)(to_next)

    def finish(i, _):
        for w in range(windows):
            change = prolong_rows(newer[w, side + i] - old[w, side + i])
            for half in range(2):
                plane = u[ROUNDS, w, DEPTH + 2 * i + half] + change
                for j in range(per):
                    out[w, 2 * i + half, pl.ds(j, 8, stride=per), :] = plane[8 * j : 8 * j + 8]
        return 0

    lax.fori_loop(0, nc, finish, 0)

    for swap in [first_k, first_r, coarse_k, coarse_r] + first_u + coarse_old + coarse_chain[1:]:
        swap.sent()

    def rounds_sent(r, _):
        for w in range(windows):
            round_swap(r, w).sent()
        return 0

    lax.fori_loop(1, ROUNDS, rounds_sent, 0)
    if groups > 1:
        pl.when(group > 0)(coarse_chain[0].sent)
        pl.when(group < groups - 1)(incoming.wait_send)


def shards(count, groups, states, kappa, rate):
    windows, n, rows, lanes = states.shape
    ext = n + 2 * DEPTH
    nc = n // 2
    cext = nc + 2 * COARSE
    crows = rows // 2
    slots = 3 * windows + 4 + ROUNDS * windows
    f32 = jnp.float32
    vmem = pl.BlockSpec(memory_space=pltpu.VMEM)
    return pl.pallas_call(
        functools.partial(kernel, count, groups),
        out_shape=jax.ShapeDtypeStruct(states.shape, f32),
        in_specs=[vmem] * 3,
        out_specs=vmem,
        scratch_shapes=[
            pltpu.VMEM((ROUNDS + 1, windows, ext, rows, lanes), f32),
            pltpu.VMEM((2, ext, rows, lanes), f32),
            pltpu.VMEM((windows, 2, DEPTH, rows, lanes), f32),
            pltpu.VMEM((2, DEPTH, rows, lanes), f32),
            pltpu.VMEM((2, max(DEPTH - 1, 1), rows, lanes), f32),
            pltpu.VMEM((ext, rows, lanes), f32),
            pltpu.VMEM((ext, rows, lanes), f32),
            pltpu.VMEM((8, ext, rows, lanes), f32),
            pltpu.VMEM((cext, crows, lanes), f32),
            pltpu.VMEM((cext, crows, lanes), f32),
            pltpu.VMEM((8, cext, crows, lanes), f32),
            pltpu.VMEM((2, cext, crows, lanes), f32),
            pltpu.VMEM((windows, cext, crows, lanes), f32),
            pltpu.VMEM((windows, cext, crows, lanes), f32),
            pltpu.VMEM((windows, cext, crows, lanes), f32),
            pltpu.VMEM((windows, cext, crows, lanes), f32),
            pltpu.VMEM((nc, crows, lanes), f32),
            pltpu.VMEM((nc, crows, lanes), f32),
            pltpu.SemaphoreType.DMA((slots, 2)),
            pltpu.SemaphoreType.DMA((slots, 2)),
            pltpu.SemaphoreType.DMA,
            pltpu.SemaphoreType.DMA,
        ],
        compiler_params=pltpu.CompilerParams(
            collective_id=0, has_side_effects=True, vmem_limit_bytes=40 * 1024 * 1024
        ),
    )(states, kappa, rate)


def solution(mesh):
    in_specs = (P("tm", "space", None, None), P("space", None, None), P("space", None, None))
    out_specs = P("tm", "space", None, None)
    body = functools.partial(shards, mesh.shape["space"], mesh.shape["tm"])
    return jax.shard_map(body, mesh=mesh, in_specs=in_specs, out_specs=out_specs, check_vma=False)
```

time: 177 us -> 58.8 us (0.33)
  the two profiles are of different devices: /device:TPU:26 before, /device:TPU:19 now
where the time goes in v1:
time: 58.8 us; the launch traced here: 58.6 us
  Pallas kernels  54.9 us (93%)
  local copies, waits for them, and re-layouts  3.74 us (6%)
    pallas_call x1, Pallas kernels, shards(): pl.pallas_call(functools.partial(kernel, count, groups), out_shape=jax.Sh...  54.9 us
    unnamed x7, local copies, waits for them, and re-layouts  3.74 us

profile of v1, /device:TPU:19, one launch (start us, length us, event | category | flops | bytes accessed | tf_op | source)
XLA Modules:
  0.0 58.6 jit_solution(18097949478075480742)
XLA Ops:
  0.0 0.0 copy-start
  0.0 1.0 %copy-done = f32[2,8,64,128]{3,2,1,0:T(8,128)S(1)} copy-done((f32[2,8,64,128]{3,2,1,0:T(8,128)S(1)}, f32[2,8,64,128]{3,2,1,0:T(8,128)}, u32[]{:S(2)}) %copy-start) | copy-done | bytes 524312
  1.0 0.0 copy-start.1
  1.0 0.9 %copy-done.1 = f32[8,64,128]{2,1,0:T(8,128)S(1)} copy-done((f32[8,64,128]{2,1,0:T(8,128)S(1)}, f32[8,64,128]{2,1,0:T(8,128)}, u32[]{:S(2)}) %copy-start.1) | copy-done | bytes 262168
  2.0 0.0 copy-start.2
  2.0 0.9 %copy-done.2 = f32[8,64,128]{2,1,0:T(8,128)S(1)} copy-done((f32[8,64,128]{2,1,0:T(8,128)S(1)}, f32[8,64,128]{2,1,0:T(8,128)}, u32[]{:S(2)}) %copy-start.2) | copy-done | bytes 262168
  2.9 54.9 %shard_map.37 = f32[2,8,64,128]{3,2,1,0:T(8,128)S(1)} custom-call(f32[2,8,64,128]{3,2,1,0:T(8,128)S(1)} %copy-done, f32[8,64,128]{2,1,0:T(8,128)S(1)} %copy-done.1, f32[8,64,128]{2,1,0:T(8,128)S(1)} %copy-done.2), custom_call_target="tpu_custom_call" | custom-call | tf_op jit(solution)/shard_map/pallas_call | solution.py:409
  57.8 0.8 %copy.5 = f32[2,8,64,128]{3,2,1,0:T(8,128)} copy(f32[2,8,64,128]{3,2,1,0:T(8,128)S(1)} %shard_map.37) | data formatting | bytes 1048576
Async XLA Ops:
  0.0 1.0 %copy-start = (f32[2,8,64,128]{3,2,1,0:T(8,128)S(1)}, f32[2,8,64,128]{3,2,1,0:T(8,128)}, u32[]{:S(2)}) copy-start(f32[2,8,64,128]{3,2,1,0:T(8,128)} %states.1) | copy-start | bytes 1572868
  1.0 0.9 %copy-start.1 = (f32[8,64,128]{2,1,0:T(8,128)S(1)}, f32[8,64,128]{2,1,0:T(8,128)}, u32[]{:S(2)}) copy-start(f32[8,64,128]{2,1,0:T(8,128)} %kappa.1) | copy-start | bytes 786436
  2.0 0.9 %copy-start.2 = (f32[8,64,128]{2,1,0:T(8,128)S(1)}, f32[8,64,128]{2,1,0:T(8,128)}, u32[]{:S(2)}) copy-start(f32[8,64,128]{2,1,0:T(8,128)} %rate.1) | copy-start | bytes 786436

commit v2 on v1

--- a/solution.py
+++ b/solution.py
@@ -12,7 +12,7 @@
 DEPTH = 2
 ROUNDS = STEPS // DEPTH
 MESH = pl.DeviceIdType.MESH
-A, R, XP, XM, YP, YM, ZP, ZM = range(8)
+A, R, XP, YP, ZP = range(5)
 
 
 def y_next(plane):
@@ -47,8 +47,7 @@
 def make_coefs(coef, field, reaction, low, high, stride, row_valid):
     rows, lanes = field.shape[-2:]
     y_up, y_down, z_up, z_down = edge_masks(rows, lanes, stride)
-
-    def body(i, _):
+    for i in range(low, high):
         k = field[i]
         r = reaction[i]
         valid = row_valid(i)
@@ -60,28 +59,29 @@
         zm = 0.5 * (k + z_prev(k, stride) * z_down)
         coef[A, i] = (1.0 + r - ((xp + xm) + (yp + ym) + (zp + zm))) * valid
         coef[R, i] = r * valid
-        coef[XP, i] = xp * valid
-        coef[XM, i] = xm * valid
-        coef[YP, i] = yp * y_up * valid
-        coef[YM, i] = ym * y_down * valid
-        coef[ZP, i] = zp * z_up * valid
-        coef[ZM, i] = zm * z_down * valid
-        return 0
-
-    lax.fori_loop(low, high, body, 0)
+        coef[XP, i] = xp * (valid * row_valid(i + 1))
+        coef[YP, i] = yp * (y_up * valid)
+        coef[ZP, i] = zp * (z_up * valid)
+
+
+def first_face(coef, field, low, row_valid):
+    both = row_valid(low) * row_valid(low + 1)
+    coef[XP, low] = (0.5 * both) * (field[low] + field[low + 1])
 
 
 def grid_step(source, target, coef, low, high, stride):
-    def body(i, _):
-        u = source[i]
+    before, u, before_face = source[low - 1], source[low], coef[XP, low - 1]
+    for i in range(low, high):
+        after = source[i + 1]
+        face = coef[XP, i]
+        y_face = coef[YP, i]
+        z_face = coef[ZP, i]
         total = u * (coef[A, i] - coef[R, i] * (u * u))
-        total = total + (coef[XP, i] * source[i + 1] + coef[XM, i] * source[i - 1])
-        total = total + (coef[YP, i] * y_next(u) + coef[YM, i] * y_prev(u))
-        total = total + (coef[ZP, i] * z_next(u, stride) + coef[ZM, i] * z_prev(u, stride))
+        total = total + (face * after + before_face * before)
+        total = total + (y_face * y_next(u) + y_prev(y_face * u))
+        total = total + (z_face * z_next(u, stride) + z_prev(z_face * u, stride))
         target[i] = total
-        return 0
-
-    lax.fori_loop(low, high, body, 0)
+        before, u, before_face = u, after, face
 
 
 def restrict_rows(first, second):
@@ -104,9 +104,9 @@
 
 def kernel(
     count, groups, states, kappa, rate, out,
-    u, temp, raw_u, raw_k, raw_r, kx, rx, coef,
+    own_u, own_k, own_r, u, temp, raw_u, raw_k, raw_r, kx, rx, coef,
     kc, rc, ccoef, ctemp, cstate, old, chain, newer, passed, outgoing,
-    send, recv, tm_send, tm_recv,
+    send, recv, tm_send, tm_recv, local,
 ):
     windows, n, rows, lanes = states.shape
     ext = n + 2 * DEPTH
@@ -179,6 +179,12 @@
     def round_swap(r, w):
         return padded_swap(u.at[r, w], n, DEPTH, slot_round + r * windows + w)
 
+    loads = [
+        pltpu.make_async_copy(source, target, local.at[i])
+        for i, (source, target) in enumerate(((kappa, own_k), (rate, own_r), (states, own_u)))
+    ]
+    for load in loads:
+        load.start()
     barrier = pltpu.get_barrier_semaphore()
 
     def greet(where):
@@ -193,15 +199,6 @@
         return jnp.concatenate(
             [ref[(*index, pl.ds(j, 8, stride=per), slice(None))] for j in range(per)], axis=0
         )
-
-    def fill_own(i, _):
-        kx[DEPTH + i] = load_plane(kappa, i)
-        rx[DEPTH + i] = load_plane(rate, i)
-        for w in range(windows):
-            u[0, w, DEPTH + i] = load_plane(states, w, i)
-        return 0
-
-    lax.fori_loop(0, n, fill_own, 0)
 
     def zero(ref, low, size):
         ref[pl.ds(low, size)] = jnp.zeros((size,) + ref.shape[1:], jnp.float32)
@@ -228,6 +225,17 @@
     for swap in first_u:
         swap.start()
 
+    loads[0].wait()
+    for i in range(n):
+        kx[DEPTH + i] = load_plane(own_k, i)
+    loads[1].wait()
+    for i in range(n):
+        rx[DEPTH + i] = load_plane(own_r, i)
+    loads[2].wait()
+    for w in range(windows):
+        for i in range(n):
+            u[0, w, DEPTH + i] = load_plane(own_u, w, i)
+
     def coarse_rows(i, _):
         base = DEPTH + 2 * i
         kc[side + i] = restrict_rows(kx[base], kx[base + 1])
@@ -236,7 +244,8 @@
             cstate[w, side + i] = restrict_rows(u[0, w, base], u[0, w, base + 1])
         return 0
 
-    lax.fori_loop(0, nc, coarse_rows, 0)
+    for i in range(nc):
+        coarse_rows(i, 0)
     coarse_k.start()
     coarse_r.start()
     for swap in coarse_old:
@@ -263,6 +272,7 @@
 
     when_left(lambda: unpack_k(0, 0, DEPTH - rate_rows))
     when_right(lambda: unpack_k(1, n + DEPTH, n + DEPTH))
+    first_face(coef, kx, 0, fine_valid)
     make_coefs(coef, kx, rx, 1, DEPTH + 1, 1, fine_valid)
     make_coefs(coef, kx, rx, DEPTH + n - 1, ext - 1, 1, fine_valid)
 
@@ -294,6 +304,7 @@
 
     coarse_k.arrived()
     coarse_r.arrived()
+    first_face(ccoef, kc, 0, coarse_valid)
     make_coefs(ccoef, kc, rc, 1, cext - 1, 2, coarse_valid)
     for w in range(windows):
         coarse_old[w].arrived()
@@ -314,11 +325,8 @@
         return (ends - old[w, side + i]) + newer[w, side + i]
 
     def carry_on(w):
-        def body(i, _):
+        for i in range(nc):
             chain[w + 1, side + i] = deltas(w, i)
-            return 0
-
-        lax.fori_loop(0, nc, body, 0)
 
     def take_old():
         newer[0, pl.ds(side, nc)] = old[0, pl.ds(side, nc)]
@@ -363,11 +371,8 @@
 
     if groups > 1:
         def to_next():
-            def body(i, _):
+            for i in range(nc):
                 outgoing[i] = deltas(windows - 1, i)
-                return 0
-
-            lax.fori_loop(0, nc, body, 0)
             incoming.start()
 
         pl.when(group < groups - 1)(to_next)
@@ -381,7 +386,8 @@
                     out[w, 2 * i + half, pl.ds(j, 8, stride=per), :] = plane[8 * j : 8 * j + 8]
         return 0
 
-    lax.fori_loop(0, nc, finish, 0)
+    for i in range(nc):
+        finish(i, 0)
 
     for swap in [first_k, first_r, coarse_k, coarse_r] + first_u + coarse_old + coarse_chain[1:]:
         swap.sent()
@@ -409,9 +415,12 @@
     return pl.pallas_call(
         functools.partial(kernel, count, groups),
         out_shape=jax.ShapeDtypeStruct(states.shape, f32),
-        in_specs=[vmem] * 3,
+        in_specs=[pl.BlockSpec(memory_space=pl.ANY)] * 3,
         out_specs=vmem,
         scratch_shapes=[
+            pltpu.VMEM(states.shape, f32),
+            pltpu.VMEM(kappa.shape, f32),
+            pltpu.VMEM(rate.shape, f32),
             pltpu.VMEM((ROUNDS + 1, windows, ext, rows, lanes), f32),
             pltpu.VMEM((2, ext, rows, lanes), f32),
             pltpu.VMEM((windows, 2, DEPTH, rows, lanes), f32),
@@ -419,10 +428,10 @@
             pltpu.VMEM((2, max(DEPTH - 1, 1), rows, lanes), f32),
             pltpu.VMEM((ext, rows, lanes), f32),
             pltpu.VMEM((ext, rows, lanes), f32),
-            pltpu.VMEM((8, ext, rows, lanes), f32),
+            pltpu.VMEM((5, ext, rows, lanes), f32),
             pltpu.VMEM((cext, crows, lanes), f32),
             pltpu.VMEM((cext, crows, lanes), f32),
-            pltpu.VMEM((8, cext, crows, lanes), f32),
+            pltpu.VMEM((5, cext, crows, lanes), f32),
             pltpu.VMEM((2, cext, crows, lanes), f32),
             pltpu.VMEM((windows, cext, crows, lanes), f32),
             pltpu.VMEM((windows, cext, crows, lanes), f32),
@@ -434,9 +443,10 @@
             pltpu.SemaphoreType.DMA((slots, 2)),
             pltpu.SemaphoreType.DMA,
             pltpu.SemaphoreType.DMA,
+            pltpu.SemaphoreType.DMA((3,)),
         ],
         compiler_params=pltpu.CompilerParams(
-            collective_id=0, has_side_effects=True, vmem_limit_bytes=40 * 1024 * 1024
+            collective_id=0, has_side_effects=True, vmem_limit_bytes=60 * 1024 * 1024
         ),
     )(states, kappa, rate)
 

time: 58.8 us -> 46.9 us (0.80)
  the two profiles are of different devices: /device:TPU:19 before, /device:TPU:10 now
where the time goes in v2:
time: 46.9 us; the launch traced here: 46.7 us
  Pallas kernels  44.8 us (96%)
  local copies, waits for them, and re-layouts  1.89 us (4%)
    pallas_call x1, Pallas kernels, shards(): pl.pallas_call(functools.partial(kernel, count, groups), out_shape=jax.Sh...  44.8 us
    unnamed x1, local copies, waits for them, and re-layouts  1.89 us

profile of v2, /device:TPU:10, one launch (start us, length us, event | category | flops | bytes accessed | tf_op | source)
XLA Modules:
  0.0 46.7 jit_solution(18132582035636794034)
XLA Ops:
  0.0 44.8 %shard_map.37 = f32[2,8,64,128]{3,2,1,0:T(8,128)} custom-call(f32[2,8,64,128]{3,2,1,0:T(8,128)} %states.1, f32[8,64,128]{2,1,0:T(8,128)} %kappa.1, f32[8,64,128]{2,1,0:T(8,128)} %rate.1), custom_call_target="tpu_custom_call" | custom-call | tf_op jit(solution)/shard_map/pallas_call | solution.py:415
  44.8 1.9 %copy.5 = f32[2,8,64,128]{3,2,1,0:T(8,128)} copy(f32[2,8,64,128]{3,2,1,0:T(8,128)} %shard_map.37) | data formatting | bytes 1048576

commit v3 on v2

--- a/solution.py
+++ b/solution.py
@@ -95,6 +95,19 @@
     return (pairs + other) * 0.125
 
 
+def even_lanes(plane):
+    return lax.broadcasted_iota(jnp.int32, plane.shape, 1) % 2 == 0
+
+
+def pack(first, second):
+    return jnp.where(even_lanes(first), first, second)
+
+
+def unpack(both):
+    even = even_lanes(both)
+    return jnp.where(even, both, z_prev(both, 1)), jnp.where(even, z_next(both, 1), both)
+
+
 def prolong_rows(plane):
     rows = plane.shape[0]
     return jnp.concatenate(
@@ -105,7 +118,7 @@
 def kernel(
     count, groups, states, kappa, rate, out,
     own_u, own_k, own_r, u, temp, raw_u, raw_k, raw_r, kx, rx, coef,
-    kc, rc, ccoef, ctemp, cstate, old, chain, newer, passed, outgoing,
+    kc, rc, kr, ccoef, ctemp, cstate, oldpair, old, chain, newer, passed, outgoing,
     send, recv, tm_send, tm_recv, local,
 ):
     windows, n, rows, lanes = states.shape
@@ -157,10 +170,11 @@
             ref.at[pl.ds(0, depth)], ref.at[pl.ds(width + depth, depth)], slot,
         )
 
-    slot_k, slot_r, slot_kc, slot_rc = (windows + i for i in range(4))
-    slot_old = windows + 4
-    slot_chain = 2 * windows + 4
-    slot_round = 3 * windows + 4
+    pairs = (windows + 1) // 2
+    slot_k, slot_r, slot_kr = (windows + i for i in range(3))
+    slot_old = windows + 3
+    slot_chain = slot_old + pairs
+    slot_round = slot_chain + windows
 
     def raw_swap(source, target, depth, slot):
         return Swap(
@@ -171,9 +185,8 @@
     first_u = [raw_swap(states.at[w], raw_u.at[w], DEPTH, w) for w in range(windows)]
     first_k = raw_swap(kappa, raw_k, DEPTH, slot_k)
     first_r = raw_swap(rate, raw_r, rate_rows, slot_r)
-    coarse_k = padded_swap(kc, nc, side, slot_kc)
-    coarse_r = padded_swap(rc, nc, side, slot_rc)
-    coarse_old = [padded_swap(cstate.at[w], nc, side, slot_old + w) for w in range(windows)]
+    coarse_kr = padded_swap(kr, nc, side, slot_kr)
+    coarse_old = [padded_swap(cstate.at[p], nc, side, slot_old + p) for p in range(pairs)]
     coarse_chain = [padded_swap(chain.at[w], nc, side, slot_chain + w) for w in range(windows)]
 
     def round_swap(r, w):
@@ -206,10 +219,10 @@
     def zero_side(fine_low, coarse_low):
         zero(kx, fine_low, DEPTH)
         zero(rx, fine_low, DEPTH)
-        zero(kc, coarse_low, side)
-        zero(rc, coarse_low, side)
+        zero(kr, coarse_low, side)
+        for p in range(pairs):
+            zero(cstate.at[p], coarse_low, side)
         for w in range(windows):
-            zero(cstate.at[w], coarse_low, side)
             zero(chain.at[w], coarse_low, side)
             for r in range(ROUNDS):
                 zero(u.at[r, w], fine_low, DEPTH)
@@ -236,18 +249,18 @@
         for i in range(n):
             u[0, w, DEPTH + i] = load_plane(own_u, w, i)
 
-    def coarse_rows(i, _):
+    for i in range(nc):
         base = DEPTH + 2 * i
         kc[side + i] = restrict_rows(kx[base], kx[base + 1])
         rc[side + i] = 4.0 * restrict_rows(rx[base], rx[base + 1])
-        for w in range(windows):
-            cstate[w, side + i] = restrict_rows(u[0, w, base], u[0, w, base + 1])
-        return 0
-
-    for i in range(nc):
-        coarse_rows(i, 0)
-    coarse_k.start()
-    coarse_r.start()
+        kr[side + i] = pack(kc[side + i], rc[side + i])
+        for p in range(pairs):
+            first, second = 2 * p, min(2 * p + 1, windows - 1)
+            cstate[p, side + i] = pack(
+                restrict_rows(u[0, first, base], u[0, first, base + 1]),
+                restrict_rows(u[0, second, base], u[0, second, base + 1]),
+            )
+    coarse_kr.start()
     for swap in coarse_old:
         swap.start()
 
@@ -259,7 +272,25 @@
         place = me * nc + i - side
         return jnp.where((place >= 0) & (place < count * nc), 1.0, 0.0)
 
+    def fine_rows(r, w, spans):
+        source = u.at[r, w]
+        for k in range(1, DEPTH + 1):
+            target = u.at[r + 1, w] if k == DEPTH else temp.at[w, k % 2]
+            for low, high in spans(k):
+                if low < high:
+                    grid_step(source, target, coef, low, high, 1)
+            source = target
+
+    def inner(r, w):
+        fine_rows(r, w, lambda k: [(DEPTH + k, n + DEPTH - k)])
+
+    def outer(r, w):
+        fine_rows(r, w, lambda k: [(k, DEPTH + k), (n + DEPTH - k, ext - k)])
+
+    first_face(coef, kx, DEPTH, fine_valid)
     make_coefs(coef, kx, rx, DEPTH + 1, DEPTH + n - 1, 1, fine_valid)
+    for w in range(windows):
+        inner(0, w)
 
     first_k.arrived()
     first_r.arrived()
@@ -276,13 +307,6 @@
     make_coefs(coef, kx, rx, 1, DEPTH + 1, 1, fine_valid)
     make_coefs(coef, kx, rx, DEPTH + n - 1, ext - 1, 1, fine_valid)
 
-    def fine_round(r, w):
-        source = u.at[r, w]
-        for k in range(1, DEPTH + 1):
-            target = u.at[r + 1, w] if k == DEPTH else temp.at[k % 2]
-            grid_step(source, target, coef, k, ext - k, 1)
-            source = target
-
     def unpack_u(w, which, low):
         for i in range(DEPTH):
             u[0, w, low + i] = load_plane(raw_u, w, which, i)
@@ -291,7 +315,7 @@
         first_u[w].arrived()
         when_left(functools.partial(unpack_u, w, 0, 0))
         when_right(functools.partial(unpack_u, w, 1, n + DEPTH))
-        fine_round(0, w)
+        outer(0, w)
         if ROUNDS > 1:
             round_swap(1, w).start()
 
@@ -302,18 +326,26 @@
             source = dest
         grid_step(source, target, ccoef, COARSE, cext - COARSE, 2)
 
-    coarse_k.arrived()
-    coarse_r.arrived()
+    coarse_kr.arrived()
+    for i in list(range(side)) + list(range(nc + side, cext)):
+        kc[i], rc[i] = unpack(kr[i])
     first_face(ccoef, kc, 0, coarse_valid)
     make_coefs(ccoef, kc, rc, 1, cext - 1, 2, coarse_valid)
-    for w in range(windows):
-        coarse_old[w].arrived()
-        coarse_run(cstate.at[w], old.at[w])
+    for p in range(pairs):
+        coarse_old[p].arrived()
+        coarse_run(cstate.at[p], oldpair.at[p])
+        for i in range(side, side + nc):
+            first, second = unpack(oldpair[p, i])
+            old[2 * p, i] = first
+            if 2 * p + 1 < windows:
+                old[2 * p + 1, i] = second
 
     def middle(r, _):
         for w in range(windows):
+            inner(r, w)
+        for w in range(windows):
             round_swap(r, w).arrived()
-            fine_round(r, w)
+            outer(r, w)
             round_swap(r + 1, w).start()
         return 0
 
@@ -338,8 +370,11 @@
 
     for w in range(windows):
         if ROUNDS > 1:
+            inner(ROUNDS - 1, w)
+    for w in range(windows):
+        if ROUNDS > 1:
             round_swap(ROUNDS - 1, w).arrived()
-            fine_round(ROUNDS - 1, w)
+            outer(ROUNDS - 1, w)
         if w == 0:
             pl.when(group == 0)(take_old)
             if windows > 1:
@@ -352,7 +387,8 @@
     if groups > 1:
         def from_before():
             incoming.wait_recv()
-            chain[0, pl.ds(side, nc)] = passed[...]
+            for i in range(nc // 2):
+                chain[0, side + 2 * i], chain[0, side + 2 * i + 1] = unpack(passed[i])
             coarse_chain[0].start()
             coarse_chain[0].arrived()
             coarse_run(chain.at[0], newer.at[0])
@@ -362,7 +398,16 @@
 
         pl.when(group > 0)(from_before)
 
+    def finish(w):
+        for i in range(nc):
+            change = prolong_rows(newer[w, side + i] - old[w, side + i])
+            for half in range(2):
+                plane = u[ROUNDS, w, DEPTH + 2 * i + half] + change
+                for j in range(per):
+                    out[w, 2 * i + half, pl.ds(j, 8, stride=per), :] = plane[8 * j : 8 * j + 8]
+
     for w in range(1, windows):
+        finish(w - 1)
         coarse_chain[w].arrived()
         coarse_run(chain.at[w], newer.at[w])
         if w + 1 < windows:
@@ -371,25 +416,15 @@
 
     if groups > 1:
         def to_next():
-            for i in range(nc):
-                outgoing[i] = deltas(windows - 1, i)
+            for i in range(nc // 2):
+                outgoing[i] = pack(deltas(windows - 1, 2 * i), deltas(windows - 1, 2 * i + 1))
             incoming.start()
 
         pl.when(group < groups - 1)(to_next)
 
-    def finish(i, _):
-        for w in range(windows):
-            change = prolong_rows(newer[w, side + i] - old[w, side + i])
-            for half in range(2):
-                plane = u[ROUNDS, w, DEPTH + 2 * i + half] + change
-                for j in range(per):
-                    out[w, 2 * i + half, pl.ds(j, 8, stride=per), :] = plane[8 * j : 8 * j + 8]
-        return 0
-
-    for i in range(nc):
-        finish(i, 0)
-
-    for swap in [first_k, first_r, coarse_k, coarse_r] + first_u + coarse_old + coarse_chain[1:]:
+    finish(windows - 1)
+
+    for swap in [first_k, first_r, coarse_kr] + first_u + coarse_old + coarse_chain[1:]:
         swap.sent()
 
     def rounds_sent(r, _):
@@ -409,7 +444,8 @@
     nc = n // 2
     cext = nc + 2 * COARSE
     crows = rows // 2
-    slots = 3 * windows + 4 + ROUNDS * windows
+    pairs = (windows + 1) // 2
+    slots = 2 * windows + pairs + 3 + ROUNDS * windows
     f32 = jnp.float32
     vmem = pl.BlockSpec(memory_space=pltpu.VMEM)
     return pl.pallas_call(
@@ -422,7 +458,7 @@
             pltpu.VMEM(kappa.shape, f32),
             pltpu.VMEM(rate.shape, f32),
             pltpu.VMEM((ROUNDS + 1, windows, ext, rows, lanes), f32),
-            pltpu.VMEM((2, ext, rows, lanes), f32),
+            pltpu.VMEM((windows, 2, ext, rows, lanes), f32),
             pltpu.VMEM((windows, 2, DEPTH, rows, lanes), f32),
             pltpu.VMEM((2, DEPTH, rows, lanes), f32),
             pltpu.VMEM((2, max(DEPTH - 1, 1), rows, lanes), f32),
@@ -431,14 +467,16 @@
             pltpu.VMEM((5, ext, rows, lanes), f32),
             pltpu.VMEM((cext, crows, lanes), f32),
             pltpu.VMEM((cext, crows, lanes), f32),
+            pltpu.VMEM((cext, crows, lanes), f32),
             pltpu.VMEM((5, cext, crows, lanes), f32),
             pltpu.VMEM((2, cext, crows, lanes), f32),
+            pltpu.VMEM((pairs, cext, crows, lanes), f32),
+            pltpu.VMEM((pairs, cext, crows, lanes), f32),
             pltpu.VMEM((windows, cext, crows, lanes), f32),
             pltpu.VMEM((windows, cext, crows, lanes), f32),
             pltpu.VMEM((windows, cext, crows, lanes), f32),
-            pltpu.VMEM((windows, cext, crows, lanes), f32),
-            pltpu.VMEM((nc, crows, lanes), f32),
-            pltpu.VMEM((nc, crows, lanes), f32),
+            pltpu.VMEM((nc // 2, crows, lanes), f32),
+            pltpu.VMEM((nc // 2, crows, lanes), f32),
             pltpu.SemaphoreType.DMA((slots, 2)),
             pltpu.SemaphoreType.DMA((slots, 2)),
             pltpu.SemaphoreType.DMA,

time: 46.9 us -> 44.3 us (0.945)
  the two profiles are of different devices: /device:TPU:10 before, /device:TPU:19 now
where the time goes in v3:
time: 44.3 us; the launch traced here: 44.2 us
  Pallas kernels  42.3 us (95%)
  local copies, waits for them, and re-layouts  1.89 us (4%)
    pallas_call x1, Pallas kernels, shards(): pl.pallas_call(functools.partial(kernel, count, groups), out_shape=jax.Sh...  42.3 us
    unnamed x1, local copies, waits for them, and re-layouts  1.89 us

profile of v3, /device:TPU:19, one launch (start us, length us, event | category | flops | bytes accessed | tf_op | source)
XLA Modules:
  0.0 44.2 jit_solution(17965255221387805559)
XLA Ops:
  0.0 42.3 %shard_map.37 = f32[2,8,64,128]{3,2,1,0:T(8,128)} custom-call(f32[2,8,64,128]{3,2,1,0:T(8,128)} %states.1, f32[8,64,128]{2,1,0:T(8,128)} %kappa.1, f32[8,64,128]{2,1,0:T(8,128)} %rate.1), custom_call_target="tpu_custom_call" | custom-call | tf_op jit(solution)/shard_map/pallas_call | solution.py:451
  42.3 1.9 %copy.5 = f32[2,8,64,128]{3,2,1,0:T(8,128)} copy(f32[2,8,64,128]{3,2,1,0:T(8,128)} %shard_map.37) | data formatting | bytes 1048576

commit v4 on v3

--- a/solution.py
+++ b/solution.py
@@ -9,7 +9,7 @@
 
 STEPS = 12
 COARSE = 3
-DEPTH = 2
+DEPTH = 3
 ROUNDS = STEPS // DEPTH
 MESH = pl.DeviceIdType.MESH
 A, R, XP, YP, ZP = range(5)

time: 44.3 us -> 42.8 us (0.966)
  Pallas kernels: 42.3 us -> 40.8 us
    pallas_call x1, Pallas kernels: 42.3 us -> 40.8 us  [shards(): pl.pallas_call(functools.partial(kernel, count, groups), out_shape=jax.Sh...]
where the time goes in v4:
time: 42.8 us; the launch traced here: 42.7 us
  Pallas kernels  40.8 us (95%)
  local copies, waits for them, and re-layouts  1.89 us (4%)
    pallas_call x1, Pallas kernels, shards(): pl.pallas_call(functools.partial(kernel, count, groups), out_shape=jax.Sh...  40.8 us
    unnamed x1, local copies, waits for them, and re-layouts  1.89 us

profile of v4, /device:TPU:19, one launch (start us, length us, event | category | flops | bytes accessed | tf_op | source)
XLA Modules:
  0.0 42.7 jit_solution(2320742318320330615)
XLA Ops:
  0.0 40.8 %shard_map.37 = f32[2,8,64,128]{3,2,1,0:T(8,128)} custom-call(f32[2,8,64,128]{3,2,1,0:T(8,128)} %states.1, f32[8,64,128]{2,1,0:T(8,128)} %kappa.1, f32[8,64,128]{2,1,0:T(8,128)} %rate.1), custom_call_target="tpu_custom_call" | custom-call | tf_op jit(solution)/shard_map/pallas_call | solution.py:451
  40.8 1.9 %copy.5 = f32[2,8,64,128]{3,2,1,0:T(8,128)} copy(f32[2,8,64,128]{3,2,1,0:T(8,128)} %shard_map.37) | data formatting | bytes 1048576
